TPU v7x, 128 devices: a whole 4x4x4 slice. The times are simulated.
128 devices in a mesh: ent: 64 (over z, y, x_lo, core), rep: 2 (over x_hi).
Axes of the slice: x: 4 (x_hi: 2, x_lo: 2; x = x_hi * 2 + x_lo), y: 4, z: 4, core: 2. Of those that a mesh axis runs over, the one named last changes fastest.
Arguments:
- entity_table: bfloat16 [4, 65536, 768], P(None, 'ent'), may hold values from -6 to 6
- relation_table: bfloat16 [4, 1387, 768], replicated, may hold values from -16 to 24
- head_ids: int32 [4096], P(('rep', 'ent')), parts along dimension 0, may hold values from 0 to 65535, as said below
- relation_ids: int32 [4096], P(('rep', 'ent')), parts along dimension 0, may hold values from 0 to 1386
- order: int32 [4096], P(('rep', 'ent')), parts along dimension 0, may hold values from 0 to 2047, as said below
- tail_ids: int32 [4096], P(('rep', 'ent')), parts along dimension 0, may hold values from 0 to 65535
Outputs:
- ensemble_logprob: float32 [4096], P(('rep', 'ent')), parts along dimension 0
- member_logprob: float32 [4096, 4], P(('rep', 'ent')), parts along dimension 0
There are 2 independent parts, one for each index of `rep`. A program takes and returns all parts, laid end to end along the dimension named above; an argument that names none is the same for every part. Nothing has to cross between parts.
Inputs may be any that keep to these rules, and one draw needn't show every extreme that they name: `head_ids`: the head of query row q lies in entities 1024 * (q // 32) to 1024 * (q // 32 + 1) - 1. `order`: a permutation of the query rows of the part that lists them by non-decreasing relation id, ties in row order.
All inputs are finite; a program needn't handle non-finite values.
Results may differ from a plain program's by a relative error of at most 0.00056.
Values may be sent and summed in bfloat16 or wider, within the bound.
A program may use at most 128 MiB of HBM per device.

v0:
```python
import jax
import jax.numpy as jnp
from jax import lax
from jax.sharding import PartitionSpec as P


def complex_product(left, right):
    half_width = left.shape[-1] // 2
    left_re, left_im = (left[..., :half_width], left[..., half_width:])
    right_re, right_im = (right[..., :half_width], right[..., half_width:])
    return jnp.concatenate(
        [left_re * right_re - left_im * right_im, left_re * right_im + left_im * right_re], axis=-1
    )


def pick_columns(values, wanted):
    row_count = values.shape[1]
    match = wanted[:, None] == jnp.arange(row_count, dtype=jnp.int32)[None, :]
    return jnp.sum(jnp.where(match[None, :, :], values[:, None, :], 0.0), axis=2)


def per_device(entity_table, relation_table, head_ids, relation_ids, order, tail_ids):
    members = entity_table.shape[0]
    local_count = entity_table.shape[1]
    offset = lax.axis_index("ent") * local_count
    entity_index = jnp.arange(local_count, dtype=jnp.int32)
    head_picker = ((head_ids - offset)[:, None] == entity_index[None, :]).astype(jnp.bfloat16)
    heads = jnp.einsum("qe,med->mqd", head_picker, entity_table, preferred_element_type=jnp.float32)
    table_rows = relation_table.shape[1]
    picker = (relation_ids[:, None] == jnp.arange(table_rows, dtype=jnp.int32)[None, :]).astype(
        jnp.bfloat16
    )
    relations = jnp.einsum(
        "qr,mrd->mqd", picker, relation_table, preferred_element_type=jnp.float32
    )
    query = complex_product(heads, relations).astype(jnp.bfloat16)
    all_tails = lax.all_gather(tail_ids, "ent", axis=0, tiled=True)
    piece = lax.all_gather(query, "ent", axis=1, tiled=True)
    tail_local = all_tails - offset
    tail_match = tail_local[:, None] == entity_index[None, :]
    peak_list = []
    total_list = []
    tail_list = []
    for member in range(members):
        scores = jnp.einsum(
            "qd,ed->qe", piece[member], entity_table[member], preferred_element_type=jnp.float32
        )
        peak_vals = jnp.max(scores, axis=1)
        peak_list.append(peak_vals)
        total_list.append(jnp.sum(jnp.exp(scores - peak_vals[:, None]), axis=1))
        tail_list.append(jnp.sum(jnp.where(tail_match, scores, 0.0), axis=1))
    stats = jnp.stack([jnp.stack(peak_list), jnp.stack(total_list), jnp.stack(tail_list)])
    peak_part, total_part, tail_part = (stats[0], stats[1], stats[2])
    global_peak = lax.pmax(peak_part.astype(jnp.bfloat16), "ent").astype(peak_part.dtype)
    scaled = total_part * jnp.exp(peak_part - global_peak)
    total_sum, tail_sum = lax.psum((scaled, tail_part), "ent")
    member_all = tail_sum - (global_peak + jnp.log(total_sum))
    member_lp = pick_columns(member_all, order)
    member_logprob = member_lp.T
    top_member = jnp.max(member_logprob, axis=1)
    ensemble_logprob = top_member + jnp.log(
        jnp.mean(jnp.exp(member_logprob - top_member[:, None]), axis=1)
    )
    return (ensemble_logprob, member_logprob)


def solution(mesh):
    placed = (
        P(None, "ent", None),
        P(),
        P(("rep", "ent")),
        P(("rep", "ent")),
        P(("rep", "ent")),
        P(("rep", "ent")),
    )
    return jax.shard_map(
        per_device,
        mesh=mesh,
        in_specs=placed,
        out_specs=(P(("rep", "ent")), P(("rep", "ent"), None)),
        check_vma=False,
    )
```

profile of v0, /device:TPU:1, one launch (start us, length us, event | category | flops | bytes accessed | tf_op | source)
XLA Modules:
  0.0 935.3 jit_solution(5652276721937168987)
XLA Ops:
  7.2 0.0 all-gather.2.cloned.1.call-start
  7.2 0.7 broadcast_subtract_fusion.1
  7.9 3.9 convolution_bitcast_fusion
  11.8 5.0 fusion.14
  16.8 0.1 subtract_convert_fusion
  16.9 0.7 pad_maximum_fusion
  17.6 0.0 all-reduce.4.cloned.1.call-start
  17.7 0.6 dynamic-slice
  18.9 0.3 dynamic-update-slice
  19.2 18.7 %all-reduce = s32[2048]{0:T(1024)S(1)} all-reduce(s32[2048]{0:T(1024)S(1)} %dynamic-update-slice), channel_id=1, replica_groups=mesh['ent'=64,'rep'=2] {'ent'}, use_global_device_ids=true, to_apply=%add | all-reduce | flops 2048 | bytes 16384
  37.9 101.7 %all-gather.2.cloned.1.call-done = bf16[4,2048,768]{2,1,0:T(8,128)(2,1)} async-done(((bf16[4,32,768]{2,1,0:T(8,128)(2,1)}), bf16[4,2048,768]{2,1,0:T(8,128)(2,1)}) %all-gather.2.cloned.1.call-update) | async-done | bytes 12582928 | tf_op jit(solution)/shard_map/all_gather | solution.py:38
  139.6 9.2 fusion.27
  148.8 7.2 fusion.28
  156.0 5.6 fusion.29
  161.6 5.6 fusion.30
  167.2 271.8 %pmax.7 = bf16[4,2048]{1,0:T(4,128)(2,1)S(1)} all-reduce(bf16[4,2048]{1,0:T(4,128)(2,1)S(1)} %fusion.26), channel_id=1, replica_groups=mesh['ent'=64,'rep'=2] {'ent'}, use_global_device_ids=true, to_apply=%region_9.10 | all-reduce | flops 8192 | bytes 32768 | tf_op jit(solution)/shard_map/pmax | solution.py:54
  439.1 14.0 %exponential_reduce_fusion.3 = (f32[2048]{0:T(1024)S(1)}, f32[2048]{0:T(1024)S(1)}, f32[2048]{0:T(1024)S(1)}, f32[2048]{0:T(1024)S(1)}, f32[2048]{0:T(1024)S(1)}...) fusion(f32[2048,1024]{0,1:T(8,128)} %get-tuple-element.21, f32[2048]{0:T(1024)S(1)} %get-tuple-element.20, ...), kind=kLoop, calls=%fused_computation.5 | loop fusion | flops 35635200 | bytes 33660928 | tf_op jit(solution)/shard_map/reduce_sum | solution.py:50
  453.1 0.6 pad_maximum_fusion.1
  453.7 0.7 fusion.24
  454.4 0.1 iota_compare_fusion.1
  454.5 472.4 %all-reduce.4.cloned.1.call-done = (f32[4,2048]{1,0:T(4,128)}, f32[4,2048]{1,0:T(4,128)}) async-done(((f32[4,2048]{1,0:T(4,128)}, f32[4,2048]{1,0:T(4,128)}), (f32[4,2048]{1,0:T(4,128)}, f32[4,2048]{1,0:T(4,128)})) %all-reduce.4.cloned.1.call-update) | async-done | bytes 65552 | tf_op jit(solution)/shard_map/psum | solution.py:56
  926.9 0.8 fusion.25
  927.7 0.2 select_reduce_fusion.4
  927.9 0.5 log_add_fusion
  (22 shorter events, 0.2 us)
Async XLA Ops:
  7.2 132.4 %all-gather.2.cloned.1.call-start = ((), (), s32[]{:S(2)}) async-start(), calls=%async_computation | async-start | bytes 12779520 | tf_op jit(solution)/shard_map/all_gather | solution.py:38
  11.8 5.8 copy-start.4
  11.8 7.1 copy-start.3
  17.6 909.3 %all-reduce.4.cloned.1.call-start = ((), (), s32[]{:S(2)}) async-start(), calls=%async_computation.1 | async-start | bytes 131072 | tf_op jit(solution)/shard_map/psum | solution.py:56
  139.6 9.2 copy-start.2
  139.6 16.4 %slice-start = ((s8[6291456]{0:T(1024)(128)(4,1)}), s8[4194304]{0:T(1024)(128)(4,1)S(1)}, s32[]{:S(2)}) async-start(s8[6291456]{0:T(1024)(128)(4,1)} %bitcast.66), calls=%async_computation.2 | async-start | bytes 8388608
  148.8 7.2 slice-start.1
  439.1 15.3 %copy-start.1 = (s32[32]{0:T(128)S(1)}, s32[32]{0:T(128)}, u32[]{:S(2)}) copy-start(s32[32]{0:T(128)} %param.10) | copy-start | bytes 388
  927.9 0.6 copy-start
Sparse Core Ops, SparseCore 0:
  17.7 121.8 all-gather.1
  454.5 472.3 all-reduce.3
where the time goes:
time: 938 us; the launch traced here: 935 us
  waiting for transfers between devices  574 us (61%)
  blocking collectives  291 us (31%)
  matrix products  36.5 us (4%)
  other arithmetic  18.4 us (2%)
  between operations  14.8 us (2%)
    psum x1, waiting for transfers between devices, per_device(): total_sum, tail_sum = lax.psum((scaled, tail_part), 'ent')  472 us
    pmax x1, blocking collectives, per_device(): lax.pmax(peak_part.astype(jnp.bfloat16), 'ent').astype(peak_part.dtype)  272 us
    all_gather x1, waiting for transfers between devices, per_device(): piece = lax.all_gather(query, 'ent', axis=1, tiled=True)  102 us
    dot_general x4, matrix products, per_device(): jnp.einsum('qd,ed->qe', piece[member], entity_table[member], preferred_el...  27.6 us
  transfers between devices with their start and end apart: 2, of which 2 were waited for; matrix products, arithmetic and copies ran while one was open for 0% of the time, Pallas kernels for 0%

commit v1 on v0

v1 whole, which is shorter than its diff:
```python
import jax
import jax.numpy as jnp
from jax import lax
from jax.experimental import pallas as pl
from jax.experimental.pallas import tpu as pltpu
from jax.sharding import PartitionSpec as P

MESH = pl.DeviceIdType.MESH
F32 = jnp.float32
BF16 = jnp.bfloat16
CHUNK = 256


def complex_product(left, right):
    half_width = left.shape[-1] // 2
    left_re, left_im = (left[..., :half_width], left[..., half_width:])
    right_re, right_im = (right[..., :half_width], right[..., half_width:])
    return jnp.concatenate(
        [left_re * right_re - left_im * right_im, left_re * right_im + left_im * right_re], axis=-1
    )


PLAN = (("y", "z", True), ("z", "y", True), ("y", "z", False), ("z", "y", False))


def score_kernel(
    q_ref, tails_ref, order_ref, ent_ref, ens_ref, mem_ref,
    u, e, s0, s1, acc_m, acc_s, acc_t, tb, tv, stat, r, row, g,
    ring_send, ring_recv, x_send, x_recv, e_local, e_send, e_recv,
    t_send, t_recv, r_send, r_recv, g_send, g_recv,
):
    rows = e.shape[2]
    n_chunk = rows // CHUNK
    idx = lax.axis_index("ent")
    rep = lax.axis_index("rep")
    core = lax.rem(idx, 2)
    x = rep * 2 + lax.rem(idx // 2, 2)
    y = lax.rem(idx // 4, 4)
    z = idx // 16

    def dev(xx, yy, zz, cc):
        return {"ent": ((zz * 4 + yy) * 2 + lax.rem(xx, 2)) * 2 + cc, "rep": xx // 2}

    def wrap(v):
        return lax.rem(v + 4, 4)

    x_up, x_down = wrap(x + 1), wrap(x - 1)
    src = y * 4 + z

    for m in (2, 3, 0, 1):
        pltpu.make_async_copy(ent_ref.at[m], e.at[0, m], e_local.at[m]).start()
    for m in range(4):
        for k in range(2):
            u[m, k, y, z] = q_ref[m, 16 * k : 16 * k + 16, :]
    s1[...] = jnp.zeros_like(s1)
    acc_m[...] = jnp.zeros_like(acc_m)
    acc_s[...] = jnp.zeros_like(acc_s)
    acc_t[...] = jnp.zeros_like(acc_t)

    barrier = pltpu.get_barrier_semaphore()

    def greet(xx, cc, first):
        def step(i, carry):
            pl.semaphore_signal(
                barrier, inc=1, device_id=dev(xx, wrap(y + i // 4), wrap(z + lax.rem(i, 4)), cc), device_id_type=MESH
            )
            return carry

        lax.fori_loop(first, 16, step, 0)

    greet(x, core, 1)
    greet(x_up, core, 0)
    greet(x_down, core, 0)
    greet(x, 1 - core, 0)
    greet(rep * 2 + 1 - lax.rem(x, 2), 1 - core, 0)
    pl.semaphore_wait(barrier, 15 + 16 * 4)

    def ring_slice(m, ph, k, pos):
        axis = PLAN[m][ph]
        if ph == 0:
            return u.at[m, k, pos, z] if axis == "y" else u.at[m, k, y, pos]
        return u.at[m, k, pos] if axis == "y" else u.at[m, k, :, pos]

    def ring_copy(m, ph, k, j, offset, shift):
        axis = PLAN[m][ph]
        me = y if axis == "y" else z
        ref = ring_slice(m, ph, k, wrap(me + offset))
        to = dev(x, wrap(y + shift), z, core) if axis == "y" else dev(x, y, wrap(z + shift), core)
        return pltpu.make_async_remote_copy(
            src_ref=ref, dst_ref=ref, send_sem=ring_send.at[m, ph, k, j], recv_sem=ring_recv.at[m, ph, k, j],
            device_id=to, device_id_type=MESH,
        )

    def ring_start(m, ph, k):
        ring_copy(m, ph, k, 0, 0, 1).start()
        ring_copy(m, ph, k, 1, 0, -1).start()

    def ring_fwd(m, ph, k):
        if k % 2 == 0:
            ring_copy(m, ph, k, 0, -1, 1).wait_recv()
            ring_copy(m, ph, k, 2, -1, 1).start()
        else:
            ring_copy(m, ph, k, 1, 1, -1).wait_recv()
            ring_copy(m, ph, k, 2, 1, -1).start()

    def ring_fin(m, ph, k):
        if k % 2 == 0:
            ring_copy(m, ph, k, 1, 1, -1).wait_recv()
        else:
            ring_copy(m, ph, k, 0, -1, 1).wait_recv()
        ring_copy(m, ph, k, 2, 2, 1).wait_recv()

    def x_copy(m, k, i):
        axis = PLAN[m][1]
        offset = (0, -1, 1, 2)[i]
        pos = wrap((y if axis == "y" else z) + offset)
        a = u.at[m, k, pos] if axis == "y" else u.at[m, k, :, pos]
        b = u.at[m, k + 2, pos] if axis == "y" else u.at[m, k + 2, :, pos]
        return pltpu.make_async_remote_copy(
            src_ref=a, dst_ref=b, send_sem=x_send.at[m, i, k], recv_sem=x_recv.at[m, i, k],
            device_id=dev(x_up if k == 0 else x_down, y, z, core), device_id_type=MESH,
        )

    def e_copy(m):
        return pltpu.make_async_remote_copy(
            src_ref=ent_ref.at[m], dst_ref=e.at[1, m], send_sem=e_send.at[m], recv_sem=e_recv.at[m],
            device_id=dev(x, y, z, 1 - core), device_id_type=MESH,
        )

    for m in (2, 3):
        for k in range(2):
            ring_start(m, 0, k)
    for m in (0, 1):
        for k in range(2):
            ring_start(m, 0, k)
    for m in (2, 3, 0, 1):
        e_copy(m).start()

    pltpu.make_async_copy(tails_ref, tb.at[src, pl.ds(0, 2)], t_recv.at[0]).start()

    def tail_copy(n, xx, yy, zz):
        a, b = ((0, 2), (0, 1), (1, 1))[n], ((0, 2), (2, 1), (3, 1))[n]
        return pltpu.make_async_remote_copy(
            src_ref=tails_ref.at[pl.ds(*a)], dst_ref=tb.at[src, pl.ds(*b)], send_sem=t_send.at[n],
            recv_sem=t_recv.at[n], device_id=dev(xx, yy, zz, core), device_id_type=MESH,
        )

    def send_all(copy, n, xx, first):
        def step(i, carry):
            copy(n, xx, wrap(y + i // 4), wrap(z + lax.rem(i, 4))).start()
            return carry

        lax.fori_loop(first, 16, step, 0)

    send_all(tail_copy, 0, x, 1)
    send_all(tail_copy, 1, x_up, 0)
    send_all(tail_copy, 2, x_down, 0)

    for m in (2, 3):
        for k in range(2):
            ring_fwd(m, 0, k)
    for m in (2, 3):
        for k in range(2):
            ring_fin(m, 0, k)
            ring_start(m, 1, k)
            x_copy(m, k, 0).start()
    for m in (0, 1):
        for k in range(2):
            ring_fwd(m, 0, k)
    for m in (0, 1):
        for k in range(2):
            ring_fin(m, 0, k)
            x_copy(m, k, 0).start()
            ring_start(m, 1, k)

    for n, part in enumerate((tb.at[:, pl.ds(0, 2)], tb.at[:, pl.ds(2, 1)], tb.at[:, pl.ds(3, 1)])):
        pltpu.make_async_copy(part, part, t_recv.at[n]).wait()
    group = lax.broadcasted_iota(jnp.int32, (8, 128), 1) // 16
    for k in range(4):
        for half in range(2):
            lanes = jnp.zeros((8, 128), jnp.int32)
            for i in range(8):
                lanes = jnp.where(group == i, tb[half * 8 + i, k], lanes)
            tv[k, :, half * 128 : half * 128 + 128] = lanes

    def fwd_second(m, k):
        ring_fwd(m, 1, k)
        if m >= 2:
            x_copy(m, k, 1 if k == 0 else 2).start()

    def fin_second(m, k):
        ring_fin(m, 1, k)
        if m >= 2:
            x_copy(m, k, 2 if k == 0 else 1).start()
            x_copy(m, k, 3).start()

    def x_started(m, k):
        x_copy(m, k - 2, 0).wait_recv()
        ring_start(m, 1, k)

    def x_done(m, k):
        for i in range(4):
            x_copy(m, k - 2, i).wait_recv()

    for k in range(2):
        for m in (2, 3):
            fwd_second(m, k)

    def batch_of(t):
        first = t < 8
        m = jnp.where(first, lax.rem(t, 2) + jnp.where(t < 4, 2, 0), lax.rem(t, 4))
        k = jnp.where(first, lax.rem(t // 2, 2), 2 + (t - 8) // 4)
        return m, k

    def e_ready(m):
        pltpu.make_async_copy(ent_ref.at[m], e.at[0, m], e_local.at[m]).wait()
        e_copy(m).wait_recv()

    def stat_copy(n, xx, yy, zz):
        ks = ((0, 2), (2, 1), (3, 1))[n]
        return pltpu.make_async_remote_copy(
            src_ref=stat.at[yy // 2, pl.ds(*ks)], dst_ref=r.at[src, pl.ds(*ks)], send_sem=r_send.at[n],
            recv_sem=r_recv.at[n], device_id=dev(xx, yy, zz, core), device_id_type=MESH,
        )

    def comm(t):
        if t == 0:
            fin_second(2, 0)
            e_ready(2)
        if t == 1:
            fin_second(3, 0)
            e_ready(3)
            x_started(0, 2)
            x_started(1, 2)
        if t == 2:
            fin_second(2, 1)
            x_started(0, 3)
            x_started(1, 3)
        if t == 3:
            fin_second(3, 1)
            fwd_second(0, 0)
            fwd_second(1, 0)
        if t == 4:
            fwd_second(0, 1)
            fwd_second(1, 1)
            fin_second(0, 0)
            e_ready(0)
        if t == 5:
            fin_second(1, 0)
            e_ready(1)
        if t == 6:
            fwd_second(0, 2)
            fwd_second(1, 2)
            fin_second(0, 1)
        if t == 7:
            fin_second(1, 1)
        if t == 8:
            fwd_second(0, 3)
            fwd_second(1, 3)
            fin_second(0, 2)
        if t == 9:
            fin_second(1, 2)
            pltpu.make_async_copy(stat.at[y // 2, pl.ds(0, 2)], r.at[src, pl.ds(0, 2)], r_recv.at[0]).start()
            send_all(stat_copy, 0, x, 1)
        if t == 10:
            x_done(2, 2)
        if t == 11:
            x_done(3, 2)
        if t == 12:
            fin_second(0, 3)
        if t == 13:
            fin_second(1, 3)
            send_all(stat_copy, 1, x_down, 0)
        if t == 14:
            x_done(2, 3)
        if t == 15:
            x_done(3, 3)

    sub = lax.broadcasted_iota(jnp.int32, (8, 256), 0)

    def dot(out, m, k, c):
        j, cc = c // n_chunk, lax.rem(c, n_chunk)
        left = e[j, m, pl.ds(pl.multiple_of(cc * CHUNK, CHUNK), CHUNK), :]
        right = u[m, k].reshape(256, e.shape[3])
        out[...] = lax.dot_general(left, right, (((1,), (1,)), ((), ())), preferred_element_type=F32)

    def process(ref, k, c, fresh):
        j = c // n_chunk
        base = (idx + j * (1 - 2 * core)) * rows + lax.rem(c, n_chunk) * CHUNK
        rel = tv[k] - base - sub
        old = jnp.where(fresh, -jnp.inf, acc_m[...])
        blocks = CHUNK // 8
        tops = [ref[8 * i : 8 * i + 8, :] for i in range(4)]
        for i in range(4, blocks):
            tops[i % 4] = jnp.maximum(tops[i % 4], ref[8 * i : 8 * i + 8, :])
        top = jnp.maximum(jnp.maximum(tops[0], tops[1]), jnp.maximum(tops[2], tops[3]))
        new = jnp.maximum(old, top)
        total = jnp.where(fresh, 0.0, acc_s[...]) * jnp.exp(old - new)
        sums = [total, jnp.zeros_like(total)]
        tail = jnp.where(fresh, 0.0, acc_t[...])
        for i in range(blocks):
            v = ref[8 * i : 8 * i + 8, :]
            sums[i % 2] = sums[i % 2] + jnp.exp(v - new)
            tail = jnp.where(rel == 8 * i, v, tail)
        acc_m[...] = new
        acc_s[...] = sums[0] + sums[1]
        acc_t[...] = tail

    def finish(m, k):
        top = jnp.max(acc_m[...], axis=0, keepdims=True)
        total = jnp.sum(acc_s[...] * jnp.exp(acc_m[...] - top), axis=0, keepdims=True)
        lse = top + jnp.log(total)
        tail = jnp.sum(acc_t[...], axis=0, keepdims=True)
        for half in range(2):
            cols = slice(half * 128, half * 128 + 128)
            stat[half, k, pl.ds(m, 1), :] = lse[:, cols]
            stat[half, k, pl.ds(m + 4, 1), :] = tail[:, cols]

    last = 2 * n_chunk - 1

    def batch(t, carry):
        for j in range(16):
            pl.when(t == j)(lambda j=j: comm(j))
        m, k = batch_of(t)
        m_old, k_old = batch_of(jnp.maximum(t - 1, 0))

        def pair(i, carry):
            head = i == 0
            dot(s0, m, k, 2 * i)
            process(s1, jnp.where(head, k_old, k), jnp.where(head, last, 2 * i - 1), False)

            @pl.when(jnp.logical_and(head, t > 0))
            def _():
                finish(m_old, k_old)

            dot(s1, m, k, 2 * i + 1)
            process(s0, k, 2 * i, head)
            return carry

        lax.fori_loop(0, n_chunk, pair, 0)
        return carry

    lax.fori_loop(0, 16, batch, 0)
    process(s1, 3, last, False)
    finish(3, 3)
    send_all(stat_copy, 2, x_up, 0)

    for n, part in enumerate((r.at[:, pl.ds(0, 2)], r.at[:, pl.ds(2, 1)], r.at[:, pl.ds(3, 1)])):
        pltpu.make_async_copy(part, part, r_recv.at[n]).wait()
    lane = lax.broadcasted_iota(jnp.int32, (1, 128), 1)
    begin = (lax.rem(y, 2) * 4 + z) * 16
    packed = jnp.zeros((1, 128), F32)
    for h in range(2):
        tiles = [r[i, h] for i in range(16)] + [r[i, h + 2] for i in range(16)]
        top = tiles[0]
        tails = tiles[0]
        for tile in tiles[1:]:
            top = jnp.maximum(top, tile)
            tails = tails + tile
        total = jnp.zeros_like(top)
        for tile in tiles:
            total = total + jnp.exp(tile - top)
        value = tails[4:8, :] - (top + jnp.log(total))[0:4, :]
        value = jnp.concatenate([value, value], axis=0)
        value = pltpu.roll(value, lax.rem(128 - begin, 128), 1)
        for m in range(4):
            at = m * 32 + h * 16
            moved = value[m : m + 1, :] if at == 0 else pltpu.roll(value, at, 1)[m : m + 1, :]
            packed = jnp.where(jnp.logical_and(lane >= at, lane < at + 16), moved, packed)
    row[...] = packed

    pltpu.make_async_copy(row, g.at[idx], g_recv.at[0]).start()

    def g_step(i, carry):
        pltpu.make_async_remote_copy(
            src_ref=row, dst_ref=g.at[idx], send_sem=g_send.at[0], recv_sem=g_recv.at[0],
            device_id={"ent": lax.rem(idx + i, 64), "rep": rep}, device_id_type=MESH,
        ).start()
        return carry

    lax.fori_loop(1, 64, g_step, 0)
    pltpu.make_async_copy(g, g, g_recv.at[0]).wait()

    order = order_ref[...]
    owner = order // 32
    inside = order - owner * 32
    picked = jnp.zeros(order.shape, F32)
    for i in range(64):
        picked = jnp.where(owner == i, g[i], picked)
    lane32 = lax.broadcasted_iota(jnp.int32, order.shape, 1)
    cols = []
    for m in range(4):
        col = jnp.sum(jnp.where(lane32 == inside + m * 32, picked, 0.0), axis=1, keepdims=True)
        mem_ref[:, m : m + 1] = col
        cols.append(col)
    best = jnp.maximum(jnp.maximum(cols[0], cols[1]), jnp.maximum(cols[2], cols[3]))
    mean = sum(jnp.exp(c - best) for c in cols) * 0.25
    ens_ref[...] = best + jnp.log(mean)

    for m in range(4):
        for k in range(2):
            for j in range(3):
                ring_copy(m, 0, k, j, 0, 1).wait_send()
        for k in range(4 if PLAN[m][2] else 2):
            for j in range(3):
                ring_copy(m, 1, k, j, 0, 1).wait_send()
        for k in range(2):
            for i in range(1 if PLAN[m][2] else 4):
                x_copy(m, k, i).wait_send()
        e_copy(m).wait_send()
    for n, part in enumerate((tb.at[pl.ds(0, 15), pl.ds(0, 2)], tb.at[:, pl.ds(2, 1)], tb.at[:, pl.ds(3, 1)])):
        pltpu.make_async_copy(part, part, t_send.at[n]).wait()
    for n, part in enumerate((r.at[pl.ds(0, 15), pl.ds(0, 2)], r.at[:, pl.ds(2, 1)], r.at[:, pl.ds(3, 1)])):
        pltpu.make_async_copy(part, part, r_send.at[n]).wait()
    part = g.at[pl.ds(0, 63)]
    pltpu.make_async_copy(part, part, g_send.at[0]).wait()


def per_device(entity_table, relation_table, head_ids, relation_ids, order, tail_ids):
    members, local_count, width = entity_table.shape
    offset = lax.axis_index("ent") * local_count
    entity_index = jnp.arange(local_count, dtype=jnp.int32)
    head_picker = ((head_ids - offset)[:, None] == entity_index[None, :]).astype(BF16)
    heads = jnp.einsum("qe,med->mqd", head_picker, entity_table, preferred_element_type=F32)
    table_rows = relation_table.shape[1]
    picker = (relation_ids[:, None] == jnp.arange(table_rows, dtype=jnp.int32)[None, :]).astype(BF16)
    relations = jnp.einsum("qr,mrd->mqd", picker, relation_table, preferred_element_type=F32)
    query = complex_product(heads, relations).astype(BF16)
    tails = jnp.tile(tail_ids.reshape(2, 1, 16), (1, 1, 8))
    order_wide = jnp.broadcast_to(order[:, None], (32, 128))
    vmem = pl.BlockSpec(memory_space=pltpu.VMEM)
    dma = pltpu.SemaphoreType.DMA
    ens, mem = pl.pallas_call(
        score_kernel,
        out_shape=(jax.ShapeDtypeStruct((32, 1), F32), jax.ShapeDtypeStruct((32, 4), F32)),
        in_specs=[vmem, vmem, vmem, pl.BlockSpec(memory_space=pl.ANY)],
        out_specs=(vmem, vmem),
        scratch_shapes=[
            pltpu.VMEM((4, 4, 4, 4, 16, width), BF16),
            pltpu.VMEM((2, 4, local_count, width), BF16),
            pltpu.VMEM((CHUNK, 256), F32),
            pltpu.VMEM((CHUNK, 256), F32),
            pltpu.VMEM((8, 256), F32),
            pltpu.VMEM((8, 256), F32),
            pltpu.VMEM((8, 256), F32),
            pltpu.VMEM((16, 4, 1, 128), jnp.int32),
            pltpu.VMEM((4, 8, 256), jnp.int32),
            pltpu.VMEM((2, 4, 8, 128), F32),
            pltpu.VMEM((16, 4, 8, 128), F32),
            pltpu.VMEM((1, 128), F32),
            pltpu.VMEM((64, 1, 128), F32),
            dma((4, 2, 4, 3)),
            dma((4, 2, 4, 3)),
            dma((4, 4, 2)),
            dma((4, 4, 2)),
            dma((4,)),
            dma((4,)),
            dma((4,)),
            dma((3,)),
            dma((3,)),
            dma((3,)),
            dma((3,)),
            dma((1,)),
            dma((1,)),
        ],
        compiler_params=pltpu.CompilerParams(
            collective_id=0, has_side_effects=True, vmem_limit_bytes=40 * 1024 * 1024
        ),
        cost_estimate=pl.CostEstimate(
            flops=2 * members * 2048 * local_count * width,
            bytes_accessed=4 * members * local_count * width,
            transcendentals=members * 2048 * local_count,
        ),
        name="score_exchange",
    )(query, tails, order_wide, entity_table)
    return (ens.reshape(32), mem)


def solution(mesh):
    placed = (
        P(None, "ent", None),
        P(),
        P(("rep", "ent")),
        P(("rep", "ent")),
        P(("rep", "ent")),
        P(("rep", "ent")),
    )
    return jax.shard_map(
        per_device,
        mesh=mesh,
        in_specs=placed,
        out_specs=(P(("rep", "ent")), P(("rep", "ent"), None)),
        check_vma=False,
    )
```

time: 938 us -> 116 us (0.12)
  waiting for transfers between devices: 574 us -> 0 us
  blocking collectives: 291 us -> 0 us
  Pallas kernels: 0 us -> 101 us
  matrix products: 36.5 us -> 8.91 us
  other arithmetic: 18.4 us -> 1.36 us
  between operations: 14.8 us -> 0.7 us
    psum x1 -> x0, waiting for transfers between devices: 472 us -> none  [per_device(): total_sum, tail_sum = lax.psum((scaled, tail_part), 'ent')]
    pmax x1 -> x0, blocking collectives: 272 us -> none  [per_device(): lax.pmax(peak_part.astype(jnp.bfloat16), 'ent').astype(peak_part.dtype)]
    all_gather x1 -> x0, waiting for transfers between devices: 102 us -> none  [per_device(): piece = lax.all_gather(query, 'ent', axis=1, tiled=True)]
    pallas_call x0 -> x1, Pallas kernels: none -> 101 us  [per_device(): pl.pallas_call(score_kernel, out_shape=(jax.ShapeDtypeStruct((32, 1), F32...]
    dot_general x4 -> x0, matrix products: 27.6 us -> none  [per_device(): jnp.einsum('qd,ed->qe', piece[member], entity_table[member], preferred_el...]
    unnamed x1 -> x0, blocking collectives: 18.7 us -> none
    reduce_sum x3 -> x0, other arithmetic: 14.2 us -> none  [the longest x1 14 us: per_device(): total_list.append(jnp.sum(jnp.exp(scores - peak_vals[:, None]), axis=1))]
  transfers between devices with their start and end apart: 2 -> 0, of which waited for: 2 -> 0; matrix products, arithmetic and copies ran while one was open for 0% -> 0% of each run, Pallas kernels for 0% -> 0%
where the time goes in v1:
time: 116 us; the launch traced here: 115 us
  Pallas kernels  101 us (87%)
  matrix products  8.91 us (8%)
  local copies, waits for them, and re-layouts  3.69 us (3%)
  other arithmetic  1.36 us (1%)
    pallas_call x1, Pallas kernels, per_device(): pl.pallas_call(score_kernel, out_shape=(jax.ShapeDtypeStruct((32, 1), F32...  101 us
    dot_general x1, matrix products, per_device(): jnp.einsum('qr,mrd->mqd', picker, relation_table, preferred_element_type=...  4.98 us
    dot_general x1, matrix products, per_device(): jnp.einsum('qe,med->mqd', head_picker, entity_table, preferred_element_ty...  3.94 us
    unnamed x7, local copies, waits for them, and re-layouts  3.46 us

profile of v1, /device:TPU:1, one launch (start us, length us, event | category | flops | bytes accessed | tf_op | source)
XLA Modules:
  0.0 115.5 jit_solution(12126509818619781502)
XLA Ops:
  0.6 0.7 broadcast_subtract_fusion
  1.3 3.9 %convolution_bitcast_fusion = f32[4,32,768]{2,1,0:T(8,128)S(1)} fusion(bf16[4,1024,768]{2,1,0:T(8,128)(2,1)} %ent_ref.1, s32[32]{0:T(128)S(1)} %broadcast_subtract_fusion), kind=kOutput, calls=%fused_computation.2 | convolution fusion | flops 201359360 | bytes 6684800 | tf_op jit(solution)/shard_map/qe,med->mqd/dot_general | solution.py:424
  5.2 0.0 copy-start.1
  5.2 0.0 copy-start.2
  5.3 5.0 %fusion.2 = f32[4,32,768]{2,1,0:T(8,128)S(1)} fusion(bf16[4,1387,768]{2,0,1:T(4,128)(2,1)} %param.7, s32[32]{0:T(128)} %param.9), kind=kOutput, calls=%fused_computation.3 | convolution fusion | flops 272739680 | bytes 8915072 | tf_op jit(solution)/shard_map/qr,mrd->mqd/dot_general | solution.py:427
  10.2 0.1 subtract_convert_fusion
  10.3 0.0 copy-done.1
  10.3 0.1 broadcast_in_dim.2.order_ref
  10.4 0.0 copy-done.2
  10.4 0.1 tile.10
  10.5 0.1 tile.12.tails_ref
  10.6 0.0 copy-start
  10.6 2.8 %copy-done = bf16[4,1024,768]{2,1,0:T(8,128)(2,1)S(1)} copy-done((bf16[4,1024,768]{2,1,0:T(8,128)(2,1)S(1)}, bf16[4,1024,768]{2,1,0:T(8,128)(2,1)}, u32[]{:S(2)}) %copy-start) | copy-done | bytes 6291480
  13.4 100.8 %score_exchange.1 = (f32[32,1]{1,0:T(8,128)S(1)}, f32[32,4]{1,0:T(8,128)S(1)}) custom-call(bf16[4,32,768]{2,1,0:T(8,128)(2,1)S(1)} %pad_maximum_fusion.q_ref, s32[2,1,128]{2,1,0:T(1,128)S(1)} %tile.12.tails_ref, s32[32,128]{1,0:T(8,128)S(1)} %broadcast_in_dim.2.order_ref, bf16[4,1024,768]{2,1,0:T(8,128)(2,1)S(1)} %copy-done), custom_call_target="tpu_custom_call" | custom-call | flops 12884901888 | bytes 12582912 | tf_op jit(solution)/shard_map/score_exchange/pallas_call | solution.py:433
  114.2 0.7 copy.11
  114.9 0.6 reduce
  (2 shorter events, 0.0 us)
Async XLA Ops:
  5.2 5.1 %copy-start.1 = (s32[32]{0:T(128)S(1)}, s32[32]{0:T(128)}, u32[]{:S(2)}) copy-start(s32[32]{0:T(128)} %param.10) | copy-start | bytes 388
  5.2 5.2 %copy-start.2 = (s32[32]{0:T(128)S(1)}, s32[32]{0:T(128)}, u32[]{:S(2)}) copy-start(s32[32]{0:T(128)} %param.11) | copy-start | bytes 388
  10.6 2.8 %copy-start = (bf16[4,1024,768]{2,1,0:T(8,128)(2,1)S(1)}, bf16[4,1024,768]{2,1,0:T(8,128)(2,1)}, u32[]{:S(2)}) copy-start(bf16[4,1024,768]{2,1,0:T(8,128)(2,1)} %ent_ref.1) | copy-start | bytes 18874372

commit v2 on v1

v2 whole, which is shorter than its diff:
```python
import jax
import jax.numpy as jnp
from jax import lax
from jax.experimental import pallas as pl
from jax.experimental.pallas import tpu as pltpu
from jax.sharding import PartitionSpec as P

MESH = pl.DeviceIdType.MESH
F32 = jnp.float32
BF16 = jnp.bfloat16


def complex_product(left, right):
    half_width = left.shape[-1] // 2
    left_re, left_im = (left[..., :half_width], left[..., half_width:])
    right_re, right_im = (right[..., :half_width], right[..., half_width:])
    return jnp.concatenate(
        [left_re * right_re - left_im * right_im, left_re * right_im + left_im * right_re], axis=-1
    )


PLAN = (("y", "z", True), ("z", "y", True), ("y", "z", False), ("z", "y", False))


def score_kernel(
    q_ref, tails_ref, order_ref, ent_ref, ens_ref, mem_ref,
    u, e, s0, s1, tb, tv, stat, rx, rz, ry, g,
    ring_send, ring_recv, x_send, x_recv, e_local, e_send, e_recv,
    t_send, t_recv, stat_send, stat_recv,
):
    rows = e.shape[2]
    idx = lax.axis_index("ent")
    rep = lax.axis_index("rep")
    core = lax.rem(idx, 2)
    x_lo = lax.rem(idx // 2, 2)
    x = rep * 2 + x_lo
    y = lax.rem(idx // 4, 4)
    z = idx // 16

    def dev(xx, yy, zz, cc):
        return {"ent": ((zz * 4 + yy) * 2 + lax.rem(xx, 2)) * 2 + cc, "rep": xx // 2}

    def wrap(v):
        return lax.rem(v + 4, 4)

    def along(axis, shift):
        if axis == "x":
            return dev(wrap(x + shift), y, z, core)
        return dev(x, wrap(y + shift), z, core) if axis == "y" else dev(x, y, wrap(z + shift), core)

    pair = rep * 2 + 1 - x_lo
    others = (dev(pair, y, z, core), dev(x, y, z, 1 - core), dev(pair, y, z, 1 - core))

    def remote(src, dst, send_sem, recv_sem, to):
        return pltpu.make_async_remote_copy(
            src_ref=src, dst_ref=dst, send_sem=send_sem, recv_sem=recv_sem, device_id=to, device_id_type=MESH
        )

    barrier = pltpu.get_barrier_semaphore()
    partners = [along(axis, shift) for axis in "zy" for shift in (1, 2, 3)]
    partners += [along("x", 1), along("x", -1), others[1], others[2]]
    for partner in partners:
        pl.semaphore_signal(barrier, inc=1, device_id=partner, device_id_type=MESH)

    for m in (2, 3, 0, 1):
        pltpu.make_async_copy(ent_ref.at[m], e.at[0, m], e_local.at[m]).start()
    for m in range(4):
        for k in range(2):
            u[m, k, y, z] = q_ref[m, 16 * k : 16 * k + 16, :]
    for k in range(2):
        tb[k, y, z] = tails_ref[k]
    pl.semaphore_wait(barrier, len(partners))

    def ring_slice(m, ph, k, pos):
        axis = PLAN[m][ph]
        if ph == 0:
            return u.at[m, k, pos, z] if axis == "y" else u.at[m, k, y, pos]
        return u.at[m, k, pos] if axis == "y" else u.at[m, k, :, pos]

    def ring_copy(m, ph, k, j, offset, shift):
        axis = PLAN[m][ph]
        ref = ring_slice(m, ph, k, wrap((y if axis == "y" else z) + offset))
        return remote(ref, ref, ring_send.at[m, ph, k, j], ring_recv.at[m, ph, k, j], along(axis, shift))

    def ring_start(m, ph, k):
        ring_copy(m, ph, k, 0, 0, 1).start()
        ring_copy(m, ph, k, 1, 0, -1).start()

    def ring_fwd(m, ph, k):
        if k % 2 == 0:
            ring_copy(m, ph, k, 0, -1, 1).wait_recv()
            ring_copy(m, ph, k, 2, -1, 1).start()
        else:
            ring_copy(m, ph, k, 1, 1, -1).wait_recv()
            ring_copy(m, ph, k, 2, 1, -1).start()

    def ring_fin(m, ph, k):
        if k % 2 == 0:
            ring_copy(m, ph, k, 1, 1, -1).wait_recv()
        else:
            ring_copy(m, ph, k, 0, -1, 1).wait_recv()
        ring_copy(m, ph, k, 2, 2, 1).wait_recv()

    def x_copy(m, k, i):
        axis = PLAN[m][1]
        pos = wrap((y if axis == "y" else z) + (0, -1, 1, 2)[i])
        a = u.at[m, k, pos] if axis == "y" else u.at[m, k, :, pos]
        b = u.at[m, k + 2, pos] if axis == "y" else u.at[m, k + 2, :, pos]
        return remote(a, b, x_send.at[m, i, k], x_recv.at[m, i, k], along("x", 1 if k == 0 else -1))

    def e_copy(m):
        return remote(ent_ref.at[m], e.at[1, m], e_send.at[m], e_recv.at[m], others[1])

    def tail_copy(ph, j, offset, shift):
        ref = tb.at[pl.ds(0, 2), wrap(y + offset), z] if ph == 0 else tb.at[pl.ds(0, 2), :, wrap(z + offset)]
        return remote(ref, ref, t_send.at[ph, j], t_recv.at[ph, j], along("yz"[ph], shift))

    def tail_x(k):
        return remote(tb.at[k], tb.at[k + 2], t_send.at[2, k], t_recv.at[2, k], along("x", 1 if k == 0 else -1))

    def tail_start(ph):
        tail_copy(ph, 0, 0, 1).start()
        tail_copy(ph, 1, 0, -1).start()

    def tail_fwd(ph):
        tail_copy(ph, 0, -1, 1).wait_recv()
        tail_copy(ph, 2, -1, 1).start()

    def tail_fin(ph):
        tail_copy(ph, 1, 1, -1).wait_recv()
        tail_copy(ph, 2, 2, 1).wait_recv()

    for m in (2, 3):
        for k in range(2):
            ring_start(m, 0, k)
    tail_start(0)
    for m in (0, 1):
        for k in range(2):
            ring_start(m, 0, k)
    for m in (2, 3, 0, 1):
        e_copy(m).start()
    for m in (2, 3):
        for k in range(2):
            ring_fwd(m, 0, k)
    tail_fwd(0)
    for k in range(2):
        for m in (2, 3):
            ring_fin(m, 0, k)
            ring_start(m, 1, k)
            x_copy(m, k, 0).start()
    tail_fin(0)
    tail_start(1)
    for m in (0, 1):
        for k in range(2):
            ring_fwd(m, 0, k)
    for k in range(2):
        for m in (0, 1):
            ring_fin(m, 0, k)
            x_copy(m, k, 0).start()
            ring_start(m, 1, k)
    tail_fwd(1)

    def fwd_second(m, k):
        ring_fwd(m, 1, k)
        if m >= 2:
            x_copy(m, k, 1 if k == 0 else 2).start()

    def fin_second(m, k):
        ring_fin(m, 1, k)
        if m >= 2:
            x_copy(m, k, 2 if k == 0 else 1).start()
            x_copy(m, k, 3).start()

    def x_started(m, k):
        x_copy(m, k - 2, 0).wait_recv()
        ring_start(m, 1, k)

    def x_done(m, k):
        for i in range(4):
            x_copy(m, k - 2, i).wait_recv()

    for k in range(2):
        for m in (2, 3):
            fwd_second(m, k)
    tail_fin(1)
    for k in range(2):
        tail_x(k).start()
    for k in range(2):
        tail_x(k).wait_recv()
    group = lax.broadcasted_iota(jnp.int32, (8, 128), 1) // 16
    for k in range(4):
        for half in range(2):
            lanes = jnp.zeros((8, 128), jnp.int32)
            for i in range(8):
                lanes = jnp.where(group == i, tb[k, half * 2 + i // 4, i % 4], lanes)
            tv[k, :, half * 128 : half * 128 + 128] = lanes

    def batch_of(t):
        first = t < 8
        m = jnp.where(first, lax.rem(t, 2) + jnp.where(t < 4, 2, 0), lax.rem(t, 4))
        k = jnp.where(first, lax.rem(t // 2, 2), 2 + (t - 8) // 4)
        return m, k

    def e_ready(m):
        pltpu.make_async_copy(ent_ref.at[m], e.at[0, m], e_local.at[m]).wait()
        e_copy(m).wait_recv()

    def stat_x(k):
        return remote(
            stat.at[k + 2], rx.at[k], stat_send.at[0, k], stat_recv.at[0, k], along("x", -1 if k == 0 else 1)
        )

    def comm(t):
        if t == 0:
            fin_second(2, 0)
            e_ready(2)
        if t == 1:
            fin_second(3, 0)
            e_ready(3)
            x_started(0, 2)
            x_started(1, 2)
        if t == 2:
            fin_second(2, 1)
            x_started(0, 3)
            x_started(1, 3)
        if t == 3:
            fin_second(3, 1)
            fwd_second(0, 0)
            fwd_second(1, 0)
        if t == 4:
            fwd_second(0, 1)
            fwd_second(1, 1)
            fin_second(0, 0)
            e_ready(0)
        if t == 5:
            fin_second(1, 0)
            e_ready(1)
        if t == 6:
            fwd_second(0, 2)
            fwd_second(1, 2)
            fin_second(0, 1)
        if t == 7:
            fin_second(1, 1)
        if t == 8:
            fwd_second(0, 3)
            fwd_second(1, 3)
            fin_second(0, 2)
        if t == 9:
            fin_second(1, 2)
        if t == 10:
            x_done(2, 2)
        if t == 11:
            x_done(3, 2)
        if t == 12:
            fin_second(0, 3)
        if t == 13:
            fin_second(1, 3)
            stat_x(0).start()
        if t == 14:
            x_done(2, 3)
        if t == 15:
            x_done(3, 3)

    sub = lax.broadcasted_iota(jnp.int32, (8, 256), 0)
    blocks = rows // 8

    def dot(out, m, k):
        right = u[m, k].reshape(256, e.shape[3])
        for j in range(2):
            out[j * rows : j * rows + rows, :] = lax.dot_general(
                e[j, m], right, (((1,), (1,)), ((), ())), preferred_element_type=F32
            )

    def process(ref, m, k):
        rel = [tv[k] - (idx + j * (1 - 2 * core)) * rows - sub for j in range(2)]
        tops = [ref[8 * i : 8 * i + 8, :] for i in range(4)]
        for i in range(4, 2 * blocks):
            tops[i % 4] = jnp.maximum(tops[i % 4], ref[8 * i : 8 * i + 8, :])
        top = jnp.maximum(jnp.maximum(tops[0], tops[1]), jnp.maximum(tops[2], tops[3]))
        top = jnp.max(top, axis=0, keepdims=True)
        wide = jnp.broadcast_to(top, (8, 256))
        sums = [jnp.zeros((8, 256), F32)] * 4
        tails = [jnp.zeros((8, 256), F32)] * 2
        for i in range(2 * blocks):
            v = ref[8 * i : 8 * i + 8, :]
            sums[i % 4] = sums[i % 4] + jnp.exp(v - wide)
            j = i // blocks
            tails[j] = jnp.where(rel[j] == 8 * (i % blocks), v, tails[j])
        total = jnp.sum((sums[0] + sums[1]) + (sums[2] + sums[3]), axis=0, keepdims=True)
        lse = top + jnp.log(total)
        tail = jnp.sum(tails[0] + tails[1], axis=0, keepdims=True)
        for half in range(2):
            cols = slice(half * 128, half * 128 + 128)
            stat[k, half, pl.ds(m, 1), :] = lse[:, cols]
            stat[k, half, pl.ds(m + 4, 1), :] = tail[:, cols]

    s1[...] = jnp.zeros_like(s1)

    def batches(i, carry):
        for p in range(2):
            t = 2 * i + p
            for j in range(p, 16, 2):
                pl.when(i == j // 2)(lambda j=j: comm(j))
            m, k = batch_of(t)
            m_old, k_old = batch_of(jnp.maximum(t - 1, 0))
            dot((s0, s1)[p], m, k)
            process((s1, s0)[p], m_old, k_old)
        return carry

    lax.fori_loop(0, 8, batches, 0)
    process(s1, 3, 3)

    stat_x(1).start()
    is_lse = lax.broadcasted_iota(jnp.int32, (8, 128), 0) < 4

    def merge(tiles):
        top = tiles[0]
        total = tiles[0]
        for tile in tiles[1:]:
            top = jnp.maximum(top, tile)
            total = total + tile
        mass = jnp.exp(tiles[0] - top)
        for tile in tiles[1:]:
            mass = mass + jnp.exp(tile - top)
        return jnp.where(is_lse, top + jnp.log(mass), total)

    def stat_ring(buf, n, axis, o):
        return remote(buf.at[0], buf.at[o], stat_send.at[n, o - 1], stat_recv.at[n, o - 1], along(axis, o))

    for h in range(2):
        stat_x(h).wait_recv()
        for half in range(2):
            rz[0, h, half] = merge([stat[h, half], rx[h, half]])
    for o in (2, 1, 3):
        stat_ring(rz, 1, "z", o).start()
    for o in (1, 3, 2):
        stat_ring(rz, 1, "z", o).wait_recv()
    for h in range(2):
        for half in range(2):
            ry[0, h, half] = merge([rz[o, h, half] for o in range(4)])
    for o in (2, 1, 3):
        stat_ring(ry, 2, "y", o).start()
    for o in (1, 3, 2):
        stat_ring(ry, 2, "y", o).wait_recv()
    mine = x_lo * 2 + core
    for half in range(2):
        both = [merge([ry[o, h, half] for o in range(4)]) for h in range(2)]
        g[mine, half] = jnp.concatenate([v[4:8, :] - v[0:4, :] for v in both], axis=0)

    def g_copy(n):
        return remote(g.at[mine], g.at[mine], stat_send.at[3, n], stat_recv.at[3, n], others[n])

    for n in range(3):
        g_copy(n).start()
    order = order_ref[...]
    d = order // 32
    h = lax.rem(order // 16, 2)
    dy = lax.rem(d // 4, 4)
    lane_at = (lax.rem(dy, 2) * 4 + d // 16) * 16 + lax.rem(order, 16)
    tile_at = (lax.rem(d, 4) * 2 + dy // 2) * 2 + h
    lane = lax.broadcasted_iota(jnp.int32, order.shape, 1)
    for n in range(3):
        g_copy(n).wait_recv()
    picked = [jnp.zeros(order.shape, F32)] * 4
    for p in range(4):
        for half in range(2):
            tile = g[p, half]
            for hh in range(2):
                hit = tile_at == (p * 2 + half) * 2 + hh
                for m in range(4):
                    picked[m] = jnp.where(hit, tile[hh * 4 + m : hh * 4 + m + 1, :], picked[m])
    cols = []
    for m in range(4):
        col = jnp.sum(jnp.where(lane == lane_at, picked[m], 0.0), axis=1, keepdims=True)
        mem_ref[:, m : m + 1] = col
        cols.append(col)
    best = jnp.maximum(jnp.maximum(cols[0], cols[1]), jnp.maximum(cols[2], cols[3]))
    mean = sum(jnp.exp(c - best) for c in cols) * 0.25
    ens_ref[...] = best + jnp.log(mean)

    for m in range(4):
        for k in range(2):
            for j in range(3):
                ring_copy(m, 0, k, j, 0, 1).wait_send()
        for k in range(4 if PLAN[m][2] else 2):
            for j in range(3):
                ring_copy(m, 1, k, j, 0, 1).wait_send()
        for k in range(2):
            for i in range(1 if PLAN[m][2] else 4):
                x_copy(m, k, i).wait_send()
        e_copy(m).wait_send()
    for j in range(3):
        tail_copy(0, j, 0, 1).wait_send()
        tail_copy(1, j, 0, 1).wait_send()
        stat_ring(rz, 1, "z", j + 1).wait_send()
        stat_ring(ry, 2, "y", j + 1).wait_send()
        g_copy(j).wait_send()
    for k in range(2):
        tail_x(k).wait_send()
        stat_x(k).wait_send()


def per_device(entity_table, relation_table, head_ids, relation_ids, order, tail_ids):
    members, local_count, width = entity_table.shape
    offset = lax.axis_index("ent") * local_count
    entity_index = jnp.arange(local_count, dtype=jnp.int32)
    head_picker = ((head_ids - offset)[:, None] == entity_index[None, :]).astype(BF16)
    heads = jnp.einsum("qe,med->mqd", head_picker, entity_table, preferred_element_type=F32)
    table_rows = relation_table.shape[1]
    picker = (relation_ids[:, None] == jnp.arange(table_rows, dtype=jnp.int32)[None, :]).astype(BF16)
    relations = jnp.einsum("qr,mrd->mqd", picker, relation_table, preferred_element_type=F32)
    query = complex_product(heads, relations).astype(BF16)
    tails = jnp.tile(tail_ids.reshape(2, 1, 16), (1, 1, 8))
    order_wide = jnp.broadcast_to(order[:, None], (32, 128))
    vmem = pl.BlockSpec(memory_space=pltpu.VMEM)
    dma = pltpu.SemaphoreType.DMA
    ens, mem = pl.pallas_call(
        score_kernel,
        out_shape=(jax.ShapeDtypeStruct((32, 1), F32), jax.ShapeDtypeStruct((32, 4), F32)),
        in_specs=[vmem, vmem, vmem, pl.BlockSpec(memory_space=pl.ANY)],
        out_specs=(vmem, vmem),
        scratch_shapes=[
            pltpu.VMEM((4, 4, 4, 4, 16, width), BF16),
            pltpu.VMEM((2, 4, local_count, width), BF16),
            pltpu.VMEM((2 * local_count, 256), F32),
            pltpu.VMEM((2 * local_count, 256), F32),
            pltpu.VMEM((4, 4, 4, 1, 128), jnp.int32),
            pltpu.VMEM((4, 8, 256), jnp.int32),
            pltpu.VMEM((4, 2, 8, 128), F32),
            pltpu.VMEM((2, 2, 8, 128), F32),
            pltpu.VMEM((4, 2, 2, 8, 128), F32),
            pltpu.VMEM((4, 2, 2, 8, 128), F32),
            pltpu.VMEM((4, 2, 8, 128), F32),
            dma((4, 2, 4, 3)),
            dma((4, 2, 4, 3)),
            dma((4, 4, 2)),
            dma((4, 4, 2)),
            dma((4,)),
            dma((4,)),
            dma((4,)),
            dma((3, 3)),
            dma((3, 3)),
            dma((4, 3)),
            dma((4, 3)),
        ],
        compiler_params=pltpu.CompilerParams(
            collective_id=0, has_side_effects=True, vmem_limit_bytes=58 * 1024 * 1024
        ),
        cost_estimate=pl.CostEstimate(
            flops=2 * members * 2048 * local_count * width,
            bytes_accessed=4 * members * local_count * width,
            transcendentals=members * 2048 * local_count,
        ),
        name="score_exchange",
    )(query, tails, order_wide, entity_table)
    return (ens.reshape(32), mem)


def solution(mesh):
    placed = (
        P(None, "ent", None),
        P(),
        P(("rep", "ent")),
        P(("rep", "ent")),
        P(("rep", "ent")),
        P(("rep", "ent")),
    )
    return jax.shard_map(
        per_device,
        mesh=mesh,
        in_specs=placed,
        out_specs=(P(("rep", "ent")), P(("rep", "ent"), None)),
        check_vma=False,
    )
```

time: 116 us -> 87.1 us (0.75)
  Pallas kernels: 101 us -> 71.1 us
  other arithmetic: 1.36 us -> 2.74 us
    pallas_call x1, Pallas kernels: 101 us -> 71.1 us  [per_device(): pl.pallas_call(score_kernel, out_shape=(jax.ShapeDtypeStruct((32, 1), F32...]
    unnamed x7 -> x5, local copies, waits for them, and re-layouts: 3.46 us -> 1.38 us
where the time goes in v2:
time: 87.1 us; the launch traced here: 86.2 us
  Pallas kernels  71.1 us (82%)
  matrix products  8.91 us (10%)
  local copies, waits for them, and re-layouts  2.79 us (3%)
  other arithmetic  2.74 us (3%)
    pallas_call x1, Pallas kernels, per_device(): pl.pallas_call(score_kernel, out_shape=(jax.ShapeDtypeStruct((32, 1), F32...  71.1 us
    dot_general x1, matrix products, per_device(): jnp.einsum('qr,mrd->mqd', picker, relation_table, preferred_element_type=...  4.98 us
    dot_general x1, matrix products, per_device(): jnp.einsum('qe,med->mqd', head_picker, entity_table, preferred_element_ty...  3.94 us

profile of v2, /device:TPU:1, one launch (start us, length us, event | category | flops | bytes accessed | tf_op | source)
XLA Modules:
  0.0 86.2 jit_solution(9886551940744539829)
XLA Ops:
  0.6 0.7 broadcast_subtract_fusion
  1.3 3.9 %convolution_bitcast_fusion = f32[4,32,768]{2,1,0:T(8,128)S(1)} fusion(bf16[4,1024,768]{2,1,0:T(8,128)(2,1)} %ent_ref.1, s32[32]{0:T(128)S(1)} %broadcast_subtract_fusion), kind=kOutput, calls=%fused_computation.2 | convolution fusion | flops 201359360 | bytes 6684800 | tf_op jit(solution)/shard_map/qe,med->mqd/dot_general | solution.py:408
  5.2 0.0 copy-start
  5.2 0.0 copy-start.1
  5.3 5.0 %fusion.2 = f32[4,32,768]{2,1,0:T(8,128)S(1)} fusion(bf16[4,1387,768]{2,0,1:T(4,128)(2,1)} %param.7, s32[32]{0:T(128)} %param.9), kind=kOutput, calls=%fused_computation.3 | convolution fusion | flops 272739680 | bytes 8915072 | tf_op jit(solution)/shard_map/qr,mrd->mqd/dot_general | solution.py:411
  10.2 0.1 subtract_convert_fusion
  10.3 0.7 pad_maximum_fusion.q_ref
  11.0 0.0 copy-done
  11.0 0.7 broadcast_in_dim.2.order_ref
  11.7 0.0 copy-done.1
  11.7 0.1 tile.10
  11.8 0.6 tile.12.tails_ref
  12.4 71.1 %score_exchange.1 = (f32[32,1]{1,0:T(8,128)}, f32[32,4]{1,0:T(8,128)}) custom-call(bf16[4,32,768]{2,1,0:T(8,128)(2,1)} %pad_maximum_fusion.q_ref, s32[2,1,128]{2,1,0:T(1,128)} %tile.12.tails_ref, s32[32,128]{1,0:T(8,128)} %broadcast_in_dim.2.order_ref, bf16[4,1024,768]{2,1,0:T(8,128)(2,1)} %ent_ref.1), custom_call_target="tpu_custom_call" | custom-call | flops 12884901888 | bytes 12582912 | tf_op jit(solution)/shard_map/score_exchange/pallas_call | solution.py:417
  83.5 1.4 %copy.11 = f32[32,4]{0,1:T(4,128)} copy(f32[32,4]{1,0:T(8,128)} %get-tuple-element.9) | data formatting | bytes 1024
  84.8 1.3 %reduce = f32[32]{0:T(128)} reduce(f32[32,1]{1,0:T(8,128)} %get-tuple-element.4, f32[]{:T(128)} %constant.12), dimensions={1}, to_apply=%get-tuple-element.4.reduce_sub_computation | reduce | bytes 260 | tf_op jit(solution)/shard_map/score_exchange/pallas_call | solution.py:417
  (1 shorter events, 0.0 us)
Async XLA Ops:
  5.2 5.8 %copy-start = (s32[32]{0:T(128)S(1)}, s32[32]{0:T(128)}, u32[]{:S(2)}) copy-start(s32[32]{0:T(128)} %param.10) | copy-start | bytes 388
  5.2 6.4 %copy-start.1 = (s32[32]{0:T(128)S(1)}, s32[32]{0:T(128)}, u32[]{:S(2)}) copy-start(s32[32]{0:T(128)} %param.11) | copy-start | bytes 388

commit v3 on v0

v3 whole, which is shorter than its diff:
```python
import jax
import jax.numpy as jnp
from jax import lax
from jax.experimental import pallas as pl
from jax.experimental.pallas import tpu as pltpu
from jax.sharding import PartitionSpec as P

MESH = pl.DeviceIdType.MESH
F32 = jnp.float32
BF16 = jnp.bfloat16

AXES = ("yz", "zy", "yz", "zy")
BATCH_M = (2, 3, 2, 3, 0, 1, 0, 1, 2, 2, 0, 1, 0, 1, 3, 3)
BATCH_K = (0, 0, 1, 1, 0, 0, 1, 1, 2, 3, 2, 2, 3, 3, 2, 3)
N_MSG = 160


def lookup(table, t):
    low = sum(v << (2 * i) for i, v in enumerate(table[:8]))
    high = sum(v << (2 * i) for i, v in enumerate(table[8:]))
    return (jnp.where(t < 8, low, high) >> (2 * lax.rem(t, 8))) & 3


def score_kernel(
    q_ref, tails_ref, order_ref, ent_ref, ens_ref, mem_ref,
    u, e, s0, s1, tb, tv, stat, r, row, g,
    send, recv, e_local, e_send, e_recv, r_send, r_recv, g_send, g_recv,
):
    rows, width = e.shape[2:]
    idx = lax.axis_index("ent")
    rep = lax.axis_index("rep")
    core = lax.rem(idx, 2)
    x_lo = lax.rem(idx // 2, 2)
    x = rep * 2 + x_lo
    y = lax.rem(idx // 4, 4)
    z = idx // 16
    src = y * 4 + z

    def dev(xx, yy, zz, cc):
        return {"ent": ((zz * 4 + yy) * 2 + lax.rem(xx, 2)) * 2 + cc, "rep": xx // 2}

    def wrap(v):
        return lax.rem(v + 4, 4)

    def along(axis, shift):
        if axis == "x":
            return dev(wrap(x + shift), y, z, core)
        return dev(x, wrap(y + shift), z, core) if axis == "y" else dev(x, y, wrap(z + shift), core)

    def remote(a, b, send_sem, recv_sem, to):
        return pltpu.make_async_remote_copy(
            src_ref=a, dst_ref=b, send_sem=send_sem, recv_sem=recv_sem, device_id=to, device_id_type=MESH
        )

    def e_own(m):
        return pltpu.make_async_copy(ent_ref.at[m], e.at[0, m], e_local.at[m])

    def e_copy(m):
        return remote(ent_ref.at[m], e.at[1, m], e_send.at[m], e_recv.at[m], dev(x, y, z, 1 - core))

    for m in (2, 3, 0, 1):
        e_own(m).start()

    barrier = pltpu.get_barrier_semaphore()
    partners = [along(axis, shift) for axis in "xyz" for shift in (1, -1)] + [dev(x, y, z, 1 - core)]
    for partner in partners:
        pl.semaphore_signal(barrier, inc=1, device_id=partner, device_id_type=MESH)

    for m in range(4):
        for k in range(2):
            u[m, k, y, z] = q_ref[m, 16 * k : 16 * k + 16, :]
    for k in range(2):
        tb[k, y, z] = tails_ref[k]
    pl.semaphore_wait(barrier, len(partners))

    numbers = {}
    sent = {}

    def sem_of(key):
        return numbers.setdefault(key, len(numbers))

    def at(m, k, first, second):
        return u.at[m, k, first, second] if AXES[m][0] == "y" else u.at[m, k, second, first]

    def own(m, ph):
        return y if AXES[m][ph] == "y" else z

    def piece(m, q):
        return slice(None) if q is None else wrap(own(m, 0) + q)

    def ring(m, ph, k, q, j):
        offset, shift = ((0, 1), (0, -1), (-1, 1) if k % 2 == 0 else (1, -1))[j]
        pos = wrap(own(m, ph) + offset)
        ref = at(m, k, pos, own(m, 1)) if ph == 0 else at(m, k, piece(m, q), pos)
        n = sem_of((m, ph, k, q, j))
        return remote(ref, ref, send.at[n], recv.at[n], along(AXES[m][ph], shift))

    def cross(m, k, q, i):
        pos = wrap(own(m, 1) + i)
        n = sem_of((m, k, q, i))
        return remote(
            at(m, k, piece(m, q), pos), at(m, k + 2, piece(m, q), pos), send.at[n], recv.at[n],
            along("x", 1 if k == 0 else -1),
        )

    def tail_ring(ph, j):
        offset, shift = ((0, 1), (0, -1), (-1, 1))[j]
        ref = tb.at[pl.ds(0, 2), wrap(y + offset), z] if ph == 0 else tb.at[pl.ds(0, 2), :, wrap(z + offset)]
        n = sem_of(("tail", ph, j))
        return remote(ref, ref, send.at[n], recv.at[n], along("yz"[ph], shift))

    def tail_cross(k):
        n = sem_of(("tail", k))
        return remote(tb.at[k], tb.at[k + 2], send.at[n], recv.at[n], along("x", 1 if k == 0 else -1))

    def start(make, *args):
        make(*args).start()
        sent[(make, args)] = True

    def arrived(make, *args):
        make(*args).wait_recv()

    def ring_start(m, ph, k, q=None):
        start(ring, m, ph, k, q, 0)
        start(ring, m, ph, k, q, 1)

    def ring_fwd(m, ph, k, q=None):
        arrived(ring, m, ph, k, q, k % 2)
        start(ring, m, ph, k, q, 2)

    def ring_fin(m, ph, k, q=None):
        arrived(ring, m, ph, k, q, 1 - k % 2)
        arrived(ring, m, ph, k, q, 2)

    for m in (2, 3, 0, 1):
        if m == 0:
            for j in range(2):
                start(tail_ring, 0, j)
        for k in range(2):
            ring_start(m, 0, k)
        for k in range(2):
            if m >= 2:
                ring_start(m, 1, k, 0)
            start(cross, m, k, 0, 0)
    for m in (2, 3, 0, 1):
        e_copy(m).start()

    def second(m, k, q):
        if m >= 2:
            ring_start(m, 1, k, q)
        start(cross, m, k, q, 0)

    for m in (2, 3, 0, 1):
        for k in range(2):
            ring_fwd(m, 0, k)
            second(m, k, -1 if k == 0 else 1)
        for k in range(2):
            arrived(ring, m, 0, k, None, 1 - k)
            second(m, k, 1 if k == 0 else -1)
    arrived(tail_ring, 0, 0)
    start(tail_ring, 0, 2)
    for m in (2, 3):
        for k in range(2):
            ring_fwd(m, 1, k, 0)
    for m in (2, 3, 0, 1):
        for k in range(2):
            arrived(ring, m, 0, k, None, 2)
            second(m, k, 2)
    arrived(tail_ring, 0, 1)
    arrived(tail_ring, 0, 2)
    for j in range(2):
        start(tail_ring, 1, j)
    for k in range(2):
        for m in (2, 3):
            ring_fwd(m, 1, k, -1)
            ring_fwd(m, 1, k, 1)
    for k in range(2):
        for m in (0, 1):
            ring_start(m, 1, k)
    arrived(tail_ring, 1, 0)
    start(tail_ring, 1, 2)
    for k in range(2):
        for m in (2, 3):
            ring_fwd(m, 1, k, 2)
    arrived(tail_ring, 1, 1)
    arrived(tail_ring, 1, 2)
    for k in range(2):
        start(tail_cross, k)

    def second_done(m, k):
        for q in (0, -1, 1, 2):
            ring_fin(m, 1, k, q)
        for i in (-1, 1, 2):
            start(cross, m, k, None, i)

    def crossed(m, k):
        for q in (0, -1, 1, 2):
            arrived(cross, m, k - 2, q, 0)
        if m >= 2:
            for i in (-1, 1, 2):
                arrived(cross, m, k - 2, None, i)
        else:
            ring_start(m, 1, k)

    def e_ready(m):
        e_own(m).wait()
        e_copy(m).wait_recv()

    def stat_copy(n, xx, yy, zz):
        ks = ((0, 2), (2, 1), (3, 1))[n]
        return remote(
            stat.at[yy // 2, pl.ds(*ks)], r.at[src, pl.ds(*ks)], r_send.at[n], r_recv.at[n], dev(xx, yy, zz, core)
        )

    def send_all(n, xx, first):
        def step(i, carry):
            stat_copy(n, xx, wrap(y + i // 4), wrap(z + lax.rem(i, 4))).start()
            return carry

        lax.fori_loop(first, 16, step, 0)

    def comm(t):
        if t == 0:
            second_done(2, 0)
            e_ready(2)
        if t == 1:
            second_done(3, 0)
            e_ready(3)
            for k in range(2):
                arrived(tail_cross, k)
            group = lax.broadcasted_iota(jnp.int32, (8, 128), 1) // 16
            for k in range(4):
                for half in range(2):
                    lanes = jnp.zeros((8, 128), jnp.int32)
                    for i in range(8):
                        lanes = jnp.where(group == i, tb[k, half * 2 + i // 4, i % 4], lanes)
                    tv[k, :, half * 128 : half * 128 + 128] = lanes
        if t == 2:
            second_done(2, 1)
            ring_fwd(0, 1, 0)
            ring_fwd(1, 1, 0)
        if t == 3:
            second_done(3, 1)
            ring_fwd(0, 1, 1)
            ring_fwd(1, 1, 1)
        if t == 4:
            e_ready(0)
            crossed(0, 2)
            crossed(1, 2)
            ring_fin(0, 1, 0)
        if t == 5:
            e_ready(1)
            crossed(0, 3)
            crossed(1, 3)
            ring_fin(1, 1, 0)
        if t == 6:
            ring_fin(0, 1, 1)
        if t == 7:
            ring_fin(1, 1, 1)
            ring_fwd(0, 1, 2)
            ring_fwd(1, 1, 2)
        if t == 8:
            crossed(2, 2)
        if t == 9:
            ring_fwd(0, 1, 3)
            ring_fwd(1, 1, 3)
            crossed(2, 3)
        if t == 10:
            pltpu.make_async_copy(stat.at[y // 2, pl.ds(0, 2)], r.at[src, pl.ds(0, 2)], r_recv.at[0]).start()
            send_all(0, x, 1)
            ring_fin(0, 1, 2)
        if t == 11:
            ring_fin(1, 1, 2)
        if t == 12:
            ring_fin(0, 1, 3)
        if t == 13:
            ring_fin(1, 1, 3)
        if t == 14:
            crossed(3, 2)
        if t == 15:
            crossed(3, 3)

    sub = lax.broadcasted_iota(jnp.int32, (8, 256), 0)
    blocks = rows // 8

    def dot(out, m, k):
        right = u[m, k].reshape(256, width)
        for j in range(2):
            out[j * rows : j * rows + rows, :] = lax.dot_general(
                e[j, m], right, (((1,), (1,)), ((), ())), preferred_element_type=F32
            )

    def process(ref, m, k):
        rel = [tv[k] - (idx + j * (1 - 2 * core)) * rows - sub for j in range(2)]
        tops = [ref[8 * i : 8 * i + 8, :] for i in range(4)]
        for i in range(4, 2 * blocks):
            tops[i % 4] = jnp.maximum(tops[i % 4], ref[8 * i : 8 * i + 8, :])
        top = jnp.maximum(jnp.maximum(tops[0], tops[1]), jnp.maximum(tops[2], tops[3]))
        top = jnp.max(top, axis=0, keepdims=True)
        wide = jnp.broadcast_to(top, (8, 256))
        sums = [jnp.zeros((8, 256), F32)] * 4
        true = [jnp.zeros((8, 256), F32)] * 2
        for i in range(2 * blocks):
            v = ref[8 * i : 8 * i + 8, :]
            sums[i % 4] = sums[i % 4] + jnp.exp(v - wide)
            j = i // blocks
            true[j] = jnp.where(rel[j] == 8 * (i % blocks), v, true[j])
        total = jnp.sum((sums[0] + sums[1]) + (sums[2] + sums[3]), axis=0, keepdims=True)
        lse = top + jnp.log(total)
        tail = jnp.sum(true[0] + true[1], axis=0, keepdims=True)
        for half in range(2):
            cols = slice(half * 128, half * 128 + 128)
            stat[half, k, pl.ds(m, 1), :] = lse[:, cols]
            stat[half, k, pl.ds(m + 4, 1), :] = tail[:, cols]

    s1[...] = jnp.zeros_like(s1)
    tv[...] = jnp.zeros_like(tv)

    def batches(i, carry):
        for p in range(2):
            t = 2 * i + p
            for j in range(p, 16, 2):
                pl.when(i == j // 2)(lambda j=j: comm(j))
            old = jnp.maximum(t - 1, 0)
            dot((s0, s1)[p], lookup(BATCH_M, t), lookup(BATCH_K, t))
            process((s1, s0)[p], lookup(BATCH_M, old), lookup(BATCH_K, old))
        return carry

    lax.fori_loop(0, 8, batches, 0)
    send_all(1, wrap(x - 1), 0)
    process(s1, BATCH_M[15], BATCH_K[15])
    send_all(2, wrap(x + 1), 0)

    whole = (r.at[:, pl.ds(0, 2)], r.at[:, pl.ds(2, 1)], r.at[:, pl.ds(3, 1)])
    part = r.at[pl.ds(0, 15), pl.ds(0, 2)]
    pltpu.make_async_copy(whole[0], whole[0], r_recv.at[0]).wait()
    pltpu.make_async_copy(part, part, r_send.at[0]).wait()

    def reduce(k):
        tiles = [r[i, k] for i in range(16)]
        top = tiles[0]
        total = tiles[0]
        for tile in tiles[1:]:
            top = jnp.maximum(top, tile)
            total = total + tile
        mass = jnp.exp(tiles[0] - top)
        for tile in tiles[1:]:
            mass = mass + jnp.exp(tile - top)
        return top, mass, total

    near = [reduce(0), reduce(1)]
    for copies in list(sent):
        make, args = copies
        make(*args).wait_send()
    for m in range(4):
        e_copy(m).wait_send()
    lane = lax.broadcasted_iota(jnp.int32, (1, 128), 1)
    begin = (lax.rem(y, 2) * 4 + z) * 16
    packed = jnp.zeros((1, 128), F32)
    for h in range(2):
        pltpu.make_async_copy(whole[1 + h], whole[1 + h], r_recv.at[1 + h]).wait()
        top0, mass0, total0 = near[h]
        top1, mass1, total1 = reduce(h + 2)
        top = jnp.maximum(top0, top1)
        lse = top + jnp.log(mass0 * jnp.exp(top0 - top) + mass1 * jnp.exp(top1 - top))
        value = (total0 + total1)[4:8, :] - lse[0:4, :]
        value = jnp.concatenate([value, value], axis=0)
        value = pltpu.roll(value, lax.rem(128 - begin, 128), 1)
        for m in range(4):
            to = m * 32 + h * 16
            moved = value[m : m + 1, :] if to == 0 else pltpu.roll(value, to, 1)[m : m + 1, :]
            packed = jnp.where(jnp.logical_and(lane >= to, lane < to + 16), moved, packed)
    row[...] = packed

    pltpu.make_async_copy(row, g.at[idx], g_recv.at[0]).start()

    def g_step(i, carry):
        to = {"ent": lax.rem(idx + i, 64), "rep": rep}
        remote(row, g.at[idx], g_send.at[0], g_recv.at[0], to).start()
        return carry

    lax.fori_loop(1, 64, g_step, 0)
    order = order_ref[...]
    sub32 = lax.broadcasted_iota(jnp.int32, order.shape, 0)
    owner = order // 32
    inside = order - owner * 32
    lane32 = lax.broadcasted_iota(jnp.int32, order.shape, 1)
    for n in range(2):
        pltpu.make_async_copy(whole[1 + n], whole[1 + n], r_send.at[1 + n]).wait()
    part = g.at[pl.ds(0, 63)]
    pltpu.make_async_copy(part, part, g_send.at[0]).wait()
    pltpu.make_async_copy(g, g, g_recv.at[0]).wait()

    picked = jnp.zeros(order.shape, F32)
    for i in range(64):
        picked = jnp.where(owner == i, g[i], picked)
    cols = []
    for m in range(4):
        col = jnp.sum(jnp.where(lane32 == inside + m * 32, picked, 0.0), axis=1, keepdims=True)
        cols.append(col)
    best = jnp.maximum(jnp.maximum(cols[0], cols[1]), jnp.maximum(cols[2], cols[3]))
    mean = sum(jnp.exp(c - best) for c in cols) * 0.25
    diagonal = sub32 == lane32
    for m, col in enumerate(cols + [best + jnp.log(mean)]):
        line = jnp.sum(jnp.where(diagonal, col, 0.0), axis=0, keepdims=True)[:, :32]
        if m < 4:
            mem_ref[m : m + 1, :] = line
        else:
            ens_ref[...] = line


def build_kernel(
    head_ref, rel_ref, order_ref, tail_ref, ent_ref, table_ref, q_ref, tails_ref, wide_ref,
    head_rows, rel_rows, qf, sem,
):
    rows, width = ent_ref.shape[1:]
    half_width = width // 2
    offset = lax.axis_index("ent") * rows

    def fetch(i, carry):
        head = pl.multiple_of((head_ref[i] - offset) // 16 * 16, 16)
        pltpu.make_async_copy(ent_ref.at[:, pl.ds(head, 16)], head_rows.at[i], sem.at[0]).start()
        pltpu.make_async_copy(table_ref.at[rel_ref[i]], rel_rows.at[i], sem.at[1]).start()
        return carry

    lax.fori_loop(0, 32, fetch, 0, unroll=4)
    lane16 = lax.rem(lax.broadcasted_iota(jnp.int32, (1, 128), 1), 16)
    for k in range(2):
        acc = jnp.zeros((1, 128), jnp.int32)
        for i in range(16):
            acc = jnp.where(lane16 == i, tail_ref[k * 16 + i], acc)
        tails_ref[k] = acc
    for i in range(32):
        wide_ref[i : i + 1, :] = jnp.full((1, 128), order_ref[i], jnp.int32)
    pltpu.make_async_copy(rel_rows, rel_rows, sem.at[1]).wait()
    pltpu.make_async_copy(head_rows, head_rows, sem.at[0]).wait()
    sub16 = lax.broadcasted_iota(jnp.int32, (16, width), 0)

    def pick(i, carry):
        hit = sub16 == lax.rem(head_ref[i], 16)
        right = rel_rows[i].astype(F32)
        for m in range(4):
            left = jnp.sum(jnp.where(hit, head_rows[i, m].astype(F32), 0.0), axis=0, keepdims=True)
            a, b = left[:, :half_width], left[:, half_width:]
            c, d = right[m : m + 1, :half_width], right[m : m + 1, half_width:]
            qf[m, pl.ds(i, 1), :half_width] = a * c - b * d
            qf[m, pl.ds(i, 1), half_width:] = a * d + b * c
        return carry

    lax.fori_loop(0, 32, pick, 0, unroll=4)
    q_ref[...] = qf[...].astype(BF16)


def per_device(entity_table, relation_table, head_ids, relation_ids, order, tail_ids):
    members, local_count, width = entity_table.shape
    vmem = pl.BlockSpec(memory_space=pltpu.VMEM)
    smem = pl.BlockSpec(memory_space=pltpu.SMEM)
    hbm = pl.BlockSpec(memory_space=pl.ANY)
    dma = pltpu.SemaphoreType.DMA
    query, tails, order_wide = pl.pallas_call(
        build_kernel,
        out_shape=(
            jax.ShapeDtypeStruct((members, 32, width), BF16),
            jax.ShapeDtypeStruct((2, 1, 128), jnp.int32),
            jax.ShapeDtypeStruct((32, 128), jnp.int32),
        ),
        in_specs=[smem, smem, smem, smem, hbm, hbm],
        out_specs=(vmem, vmem, vmem),
        scratch_shapes=[
            pltpu.VMEM((32, members, 16, width), BF16),
            pltpu.VMEM((32, members, width), BF16),
            pltpu.VMEM((members, 32, width), F32),
            dma((2,)),
        ],
        compiler_params=pltpu.CompilerParams(vmem_limit_bytes=58 * 1024 * 1024),
        name="build_queries",
    )(head_ids, relation_ids, order, tail_ids, entity_table, jnp.transpose(relation_table, (1, 0, 2)))
    ens, mem = pl.pallas_call(
        score_kernel,
        out_shape=(jax.ShapeDtypeStruct((1, 32), F32), jax.ShapeDtypeStruct((4, 32), F32)),
        in_specs=[vmem, vmem, vmem, hbm],
        out_specs=(vmem, vmem),
        scratch_shapes=[
            pltpu.VMEM((4, 4, 4, 4, 16, width), BF16),
            pltpu.VMEM((2, 4, local_count, width), BF16),
            pltpu.VMEM((2 * local_count, 256), F32),
            pltpu.VMEM((2 * local_count, 256), F32),
            pltpu.VMEM((4, 4, 4, 1, 128), jnp.int32),
            pltpu.VMEM((4, 8, 256), jnp.int32),
            pltpu.VMEM((2, 4, 8, 128), F32),
            pltpu.VMEM((16, 4, 8, 128), F32),
            pltpu.VMEM((1, 128), F32),
            pltpu.VMEM((64, 1, 128), F32),
            dma((N_MSG,)),
            dma((N_MSG,)),
            dma((4,)),
            dma((4,)),
            dma((4,)),
            dma((3,)),
            dma((3,)),
            dma((1,)),
            dma((1,)),
        ],
        compiler_params=pltpu.CompilerParams(
            collective_id=0, has_side_effects=True, vmem_limit_bytes=58 * 1024 * 1024
        ),
        cost_estimate=pl.CostEstimate(
            flops=2 * members * 2048 * local_count * width,
            bytes_accessed=4 * members * local_count * width,
            transcendentals=members * 2048 * local_count,
        ),
        name="score_exchange",
    )(query, tails, order_wide, entity_table)
    return (ens.reshape(32), mem.T)


def solution(mesh):
    placed = (
        P(None, "ent", None),
        P(),
        P(("rep", "ent")),
        P(("rep", "ent")),
        P(("rep", "ent")),
        P(("rep", "ent")),
    )
    return jax.shard_map(
        per_device,
        mesh=mesh,
        in_specs=placed,
        out_specs=(P(("rep", "ent")), P(("rep", "ent"), None)),
        check_vma=False,
    )
```

time: 938 us -> 73.9 us (0.08)
  waiting for transfers between devices: 574 us -> 0 us
  blocking collectives: 291 us -> 0 us
  Pallas kernels: 0 us -> 70.6 us
  matrix products: 36.5 us -> 0 us
  other arithmetic: 18.4 us -> 0 us
  between operations: 14.8 us -> 0.65 us
    psum x1 -> x0, waiting for transfers between devices: 472 us -> none  [per_device(): total_sum, tail_sum = lax.psum((scaled, tail_part), 'ent')]
    pmax x1 -> x0, blocking collectives: 272 us -> none  [per_device(): lax.pmax(peak_part.astype(jnp.bfloat16), 'ent').astype(peak_part.dtype)]
    all_gather x1 -> x0, waiting for transfers between devices: 102 us -> none  [per_device(): piece = lax.all_gather(query, 'ent', axis=1, tiled=True)]
    pallas_call x0 -> x2, Pallas kernels: none -> 70.6 us  [the longest x1 65.2 us: per_device(): pl.pallas_call(score_kernel, out_shape=(jax.ShapeDtypeStruct((1, 32), F32...]
    dot_general x6 -> x0, matrix products: 36.5 us -> none  [the longest x4 27.6 us: per_device(): jnp.einsum('qd,ed->qe', piece[member], entity_table[member], preferred_el...]
    unnamed x1 -> x0, blocking collectives: 18.7 us -> none
    reduce_sum x3 -> x0, other arithmetic: 14.2 us -> none  [the longest x1 14 us: per_device(): total_list.append(jnp.sum(jnp.exp(scores - peak_vals[:, None]), axis=1))]
  transfers between devices with their start and end apart: 2 -> 0, of which waited for: 2 -> 0; matrix products, arithmetic and copies ran while one was open for 0% -> 0% of each run, Pallas kernels for 0% -> 0%
where the time goes in v3:
time: 73.9 us; the launch traced here: 73.7 us
  Pallas kernels  70.6 us (96%)
  local copies, waits for them, and re-layouts  2.42 us (3%)
    pallas_call x1, Pallas kernels, per_device(): pl.pallas_call(score_kernel, out_shape=(jax.ShapeDtypeStruct((1, 32), F32...  65.2 us
    pallas_call x1, Pallas kernels, per_device(): pl.pallas_call(build_kernel, out_shape=(jax.ShapeDtypeStruct((members, 32...  5.4 us
    unnamed x2, local copies, waits for them, and re-layouts  2.42 us

profile of v3, /device:TPU:1, one launch (start us, length us, event | category | flops | bytes accessed | tf_op | source)
XLA Modules:
  0.0 73.7 jit_solution(3770063437023129049)
XLA Ops:
  0.6 5.4 %build_queries.1 = (bf16[4,32,768]{2,1,0:T(8,128)(2,1)}, s32[2,1,128]{2,1,0:T(1,128)}, s32[32,128]{1,0:T(8,128)}) custom-call(s32[32]{0:T(128)} %head_ref.1, s32[32]{0:T(128)} %rel_ref.1, s32[32]{0:T(128)} %order_ref.1, s32[32]{0:T(128)} %tail_ref.1, bf16[4,1024,768]{2,1,0:T(8,128)(2,1)} %ent_ref.3, bf16[1387,4,768]{2,1,0:T(4,128)(2,1)} %bitcast.3), custom_call_target="tpu_custom_call" | custom-call | tf_op jit(solution)/shard_map/build_queries/pallas_call | solution.py:460
  6.0 65.2 %score_exchange.1 = (f32[1,32]{1,0:T(1,128)}, f32[4,32]{1,0:T(4,128)}) custom-call(bf16[4,32,768]{2,1,0:T(8,128)(2,1)} %get-tuple-element.7.q_ref, s32[2,1,128]{2,1,0:T(1,128)} %get-tuple-element.8.tails_ref, s32[32,128]{1,0:T(8,128)} %get-tuple-element.9.order_ref, bf16[4,1024,768]{2,1,0:T(8,128)(2,1)} %ent_ref.3), custom_call_target="tpu_custom_call" | custom-call | flops 12884901888 | bytes 12582912 | tf_op jit(solution)/shard_map/score_exchange/pallas_call | solution.py:478
  71.3 1.2 %copy.10 = f32[32]{0:T(128)} copy(f32[32]{0:T(128)} %bitcast.5) | data formatting | bytes 256
  72.5 1.2 %copy.11 = f32[32,4]{0,1:T(4,128)} copy(f32[32,4]{0,1:T(4,128)} %bitcast.4) | data formatting | bytes 1024

commit v4 on v3

--- a/solution.py
+++ b/solution.py
@@ -22,8 +22,8 @@
 
 
 def score_kernel(
-    q_ref, tails_ref, order_ref, ent_ref, ens_ref, mem_ref,
-    u, e, s0, s1, tb, tv, stat, r, row, g,
+    q_ref, tails_ref, order_ref, ent_ref, out_ref,
+    u, e, s0, s1, tb, tv, stat, rowed, r, row, g,
     send, recv, e_local, e_send, e_recv, r_send, r_recv, g_send, g_recv,
 ):
     rows, width = e.shape[2:]
@@ -174,14 +174,14 @@
         for m in (2, 3):
             ring_fwd(m, 1, k, -1)
             ring_fwd(m, 1, k, 1)
-    for k in range(2):
-        for m in (0, 1):
-            ring_start(m, 1, k)
     arrived(tail_ring, 1, 0)
     start(tail_ring, 1, 2)
     for k in range(2):
         for m in (2, 3):
             ring_fwd(m, 1, k, 2)
+            start(cross, m, k, None, -1 if k == 0 else 1)
+    for m in (0, 1):
+        ring_start(m, 1, 0)
     arrived(tail_ring, 1, 1)
     arrived(tail_ring, 1, 2)
     for k in range(2):
@@ -190,7 +190,7 @@
     def second_done(m, k):
         for q in (0, -1, 1, 2):
             ring_fin(m, 1, k, q)
-        for i in (-1, 1, 2):
+        for i in (1 if k == 0 else -1, 2):
             start(cross, m, k, None, i)
 
     def crossed(m, k):
@@ -209,8 +209,20 @@
     def stat_copy(n, xx, yy, zz):
         ks = ((0, 2), (2, 1), (3, 1))[n]
         return remote(
-            stat.at[yy // 2, pl.ds(*ks)], r.at[src, pl.ds(*ks)], r_send.at[n], r_recv.at[n], dev(xx, yy, zz, core)
+            rowed.at[yy * 4 + zz, pl.ds(*ks)], r.at[src, pl.ds(*ks)], r_send.at[n], r_recv.at[n], dev(xx, yy, zz, core)
         )
+
+    def pack(k):
+        skew = lax.rem(
+            lax.broadcasted_iota(jnp.int32, (8, 128), 1) // 16 - lax.broadcasted_iota(jnp.int32, (8, 128), 0) + 8, 8
+        )
+        for half in range(2):
+            tile = stat[half, k]
+            out = tile
+            for d in range(1, 8):
+                out = jnp.where(skew == d, pltpu.roll(pltpu.roll(tile, 8 - d, 0), 16 * d, 1), out)
+            for i in range(8):
+                rowed[half * 8 + i, k] = out[i : i + 1, :]
 
     def send_all(n, xx, first):
         def step(i, carry):
@@ -221,10 +233,13 @@
 
     def comm(t):
         if t == 0:
-            second_done(2, 0)
+            for m in (0, 1):
+                ring_start(m, 1, 1)
+            for k in range(2):
+                for m in (2, 3):
+                    second_done(m, k)
             e_ready(2)
         if t == 1:
-            second_done(3, 0)
             e_ready(3)
             for k in range(2):
                 arrived(tail_cross, k)
@@ -236,11 +251,9 @@
                         lanes = jnp.where(group == i, tb[k, half * 2 + i // 4, i % 4], lanes)
                     tv[k, :, half * 128 : half * 128 + 128] = lanes
         if t == 2:
-            second_done(2, 1)
             ring_fwd(0, 1, 0)
             ring_fwd(1, 1, 0)
         if t == 3:
-            second_done(3, 1)
             ring_fwd(0, 1, 1)
             ring_fwd(1, 1, 1)
         if t == 4:
@@ -266,7 +279,9 @@
             ring_fwd(1, 1, 3)
             crossed(2, 3)
         if t == 10:
-            pltpu.make_async_copy(stat.at[y // 2, pl.ds(0, 2)], r.at[src, pl.ds(0, 2)], r_recv.at[0]).start()
+            pack(0)
+            pack(1)
+            pltpu.make_async_copy(rowed.at[src, pl.ds(0, 2)], r.at[src, pl.ds(0, 2)], r_recv.at[0]).start()
             send_all(0, x, 1)
             ring_fin(0, 1, 2)
         if t == 11:
@@ -327,8 +342,10 @@
         return carry
 
     lax.fori_loop(0, 8, batches, 0)
+    pack(2)
     send_all(1, wrap(x - 1), 0)
     process(s1, BATCH_M[15], BATCH_K[15])
+    pack(3)
     send_all(2, wrap(x + 1), 0)
 
     whole = (r.at[:, pl.ds(0, 2)], r.at[:, pl.ds(2, 1)], r.at[:, pl.ds(3, 1)])
@@ -354,23 +371,19 @@
         make(*args).wait_send()
     for m in range(4):
         e_copy(m).wait_send()
-    lane = lax.broadcasted_iota(jnp.int32, (1, 128), 1)
-    begin = (lax.rem(y, 2) * 4 + z) * 16
-    packed = jnp.zeros((1, 128), F32)
+    def half_turn(v):
+        return pltpu.roll(jnp.broadcast_to(v, (8, 128)), 64, 1)[0:1, :]
+
+    values = []
     for h in range(2):
         pltpu.make_async_copy(whole[1 + h], whole[1 + h], r_recv.at[1 + h]).wait()
         top0, mass0, total0 = near[h]
         top1, mass1, total1 = reduce(h + 2)
         top = jnp.maximum(top0, top1)
         lse = top + jnp.log(mass0 * jnp.exp(top0 - top) + mass1 * jnp.exp(top1 - top))
-        value = (total0 + total1)[4:8, :] - lse[0:4, :]
-        value = jnp.concatenate([value, value], axis=0)
-        value = pltpu.roll(value, lax.rem(128 - begin, 128), 1)
-        for m in range(4):
-            to = m * 32 + h * 16
-            moved = value[m : m + 1, :] if to == 0 else pltpu.roll(value, to, 1)[m : m + 1, :]
-            packed = jnp.where(jnp.logical_and(lane >= to, lane < to + 16), moved, packed)
-    row[...] = packed
+        total = total0 + total1
+        values.append(half_turn(total) - lse if h == 0 else total - half_turn(lse))
+    row[...] = jnp.where(lax.broadcasted_iota(jnp.int32, (1, 128), 1) < 64, values[0], values[1])
 
     pltpu.make_async_copy(row, g.at[idx], g_recv.at[0]).start()
 
@@ -383,7 +396,7 @@
     order = order_ref[...]
     sub32 = lax.broadcasted_iota(jnp.int32, order.shape, 0)
     owner = order // 32
-    inside = order - owner * 32
+    inside = lax.rem(order // 16, 2) * 64 + lax.rem(order, 16)
     lane32 = lax.broadcasted_iota(jnp.int32, order.shape, 1)
     for n in range(2):
         pltpu.make_async_copy(whole[1 + n], whole[1 + n], r_send.at[1 + n]).wait()
@@ -396,17 +409,14 @@
         picked = jnp.where(owner == i, g[i], picked)
     cols = []
     for m in range(4):
-        col = jnp.sum(jnp.where(lane32 == inside + m * 32, picked, 0.0), axis=1, keepdims=True)
+        col = jnp.sum(jnp.where(lane32 == inside + m * 16, picked, 0.0), axis=1, keepdims=True)
         cols.append(col)
     best = jnp.maximum(jnp.maximum(cols[0], cols[1]), jnp.maximum(cols[2], cols[3]))
     mean = sum(jnp.exp(c - best) for c in cols) * 0.25
     diagonal = sub32 == lane32
+    out_ref[...] = jnp.zeros_like(out_ref)
     for m, col in enumerate(cols + [best + jnp.log(mean)]):
-        line = jnp.sum(jnp.where(diagonal, col, 0.0), axis=0, keepdims=True)[:, :32]
-        if m < 4:
-            mem_ref[m : m + 1, :] = line
-        else:
-            ens_ref[...] = line
+        out_ref[m : m + 1, :] = jnp.sum(jnp.where(diagonal, col, 0.0), axis=0, keepdims=True)
 
 
 def build_kernel(
@@ -475,11 +485,11 @@
         compiler_params=pltpu.CompilerParams(vmem_limit_bytes=58 * 1024 * 1024),
         name="build_queries",
     )(head_ids, relation_ids, order, tail_ids, entity_table, jnp.transpose(relation_table, (1, 0, 2)))
-    ens, mem = pl.pallas_call(
+    out = pl.pallas_call(
         score_kernel,
-        out_shape=(jax.ShapeDtypeStruct((1, 32), F32), jax.ShapeDtypeStruct((4, 32), F32)),
+        out_shape=jax.ShapeDtypeStruct((8, 128), F32),
         in_specs=[vmem, vmem, vmem, hbm],
-        out_specs=(vmem, vmem),
+        out_specs=vmem,
         scratch_shapes=[
             pltpu.VMEM((4, 4, 4, 4, 16, width), BF16),
             pltpu.VMEM((2, 4, local_count, width), BF16),
@@ -488,7 +498,8 @@
             pltpu.VMEM((4, 4, 4, 1, 128), jnp.int32),
             pltpu.VMEM((4, 8, 256), jnp.int32),
             pltpu.VMEM((2, 4, 8, 128), F32),
-            pltpu.VMEM((16, 4, 8, 128), F32),
+            pltpu.VMEM((16, 4, 1, 128), F32),
+            pltpu.VMEM((16, 4, 1, 128), F32),
             pltpu.VMEM((1, 128), F32),
             pltpu.VMEM((64, 1, 128), F32),
             dma((N_MSG,)),
@@ -511,7 +522,7 @@
         ),
         name="score_exchange",
     )(query, tails, order_wide, entity_table)
-    return (ens.reshape(32), mem.T)
+    return (out[4, :32], out[:4, :32].T)
 
 
 def solution(mesh):

time: 73.9 us -> 73.5 us (level)
    unnamed x2 -> x0, local copies, waits for them, and re-layouts: 2.42 us -> none
    transpose x0 -> x1, local copies, waits for them, and re-layouts: none -> 1.25 us  [per_device(): return (out[4, :32], out[:4, :32].T)]
    squeeze x0 -> x1, local copies, waits for them, and re-layouts: none -> 1.19 us  [per_device(): return (out[4, :32], out[:4, :32].T)]
where the time goes in v4:
time: 73.5 us; the launch traced here: 73.2 us
  Pallas kernels  70.1 us (95%)
  local copies, waits for them, and re-layouts  2.44 us (3%)
    pallas_call x1, Pallas kernels, per_device(): pl.pallas_call(score_kernel, out_shape=jax.ShapeDtypeStruct((8, 128), F32...  64.7 us
    pallas_call x1, Pallas kernels, per_device(): pl.pallas_call(build_kernel, out_shape=(jax.ShapeDtypeStruct((members, 32...  5.41 us

profile of v4, /device:TPU:1, one launch (start us, length us, event | category | flops | bytes accessed | tf_op | source)
XLA Modules:
  0.0 73.2 jit_solution(7618869316597011806)
XLA Ops:
  0.6 5.4 %build_queries.1 = (bf16[4,32,768]{2,1,0:T(8,128)(2,1)}, s32[2,1,128]{2,1,0:T(1,128)}, s32[32,128]{1,0:T(8,128)}) custom-call(s32[32]{0:T(128)} %head_ref.1, s32[32]{0:T(128)} %rel_ref.1, s32[32]{0:T(128)} %order_ref.1, s32[32]{0:T(128)} %tail_ref.1, bf16[4,1024,768]{2,1,0:T(8,128)(2,1)} %ent_ref.3, bf16[1387,4,768]{2,1,0:T(4,128)(2,1)} %bitcast.5), custom_call_target="tpu_custom_call" | custom-call | tf_op jit(solution)/shard_map/build_queries/pallas_call | solution.py:470
  6.0 64.7 %score_exchange.1 = f32[8,128]{1,0:T(8,128)} custom-call(bf16[4,32,768]{2,1,0:T(8,128)(2,1)} %get-tuple-element.5.q_ref, s32[2,1,128]{2,1,0:T(1,128)} %get-tuple-element.6.tails_ref, s32[32,128]{1,0:T(8,128)} %get-tuple-element.7.order_ref, bf16[4,1024,768]{2,1,0:T(8,128)(2,1)} %ent_ref.3), custom_call_target="tpu_custom_call" | custom-call | flops 12884901888 | bytes 12582912 | tf_op jit(solution)/shard_map/score_exchange/pallas_call | solution.py:488
  70.8 1.2 %slice_bitcast_fusion.1 = f32[32]{0:T(128)} fusion(f32[8,128]{1,0:T(8,128)} %score_exchange.1), kind=kLoop, calls=%fused_computation.1 | loop fusion | bytes 256 | tf_op jit(solution)/shard_map/squeeze | solution.py:525
  72.0 1.3 %slice_bitcast_fusion = f32[32,4]{0,1:T(4,128)} fusion(f32[8,128]{1,0:T(8,128)} %score_exchange.1), kind=kLoop, calls=%fused_computation | loop fusion | bytes 1024 | tf_op jit(solution)/shard_map/transpose | solution.py:525

commit v5 on v4

--- a/solution.py
+++ b/solution.py
@@ -10,8 +10,8 @@
 BF16 = jnp.bfloat16
 
 AXES = ("yz", "zy", "yz", "zy")
-BATCH_M = (2, 3, 2, 3, 0, 1, 0, 1, 2, 2, 0, 1, 0, 1, 3, 3)
-BATCH_K = (0, 0, 1, 1, 0, 0, 1, 1, 2, 3, 2, 2, 3, 3, 2, 3)
+BATCH_M = (2, 3, 2, 3, 0, 1, 0, 1, 2, 2, 0, 1, 3, 3, 0, 1)
+BATCH_K = (0, 0, 1, 1, 0, 0, 1, 1, 2, 3, 2, 2, 2, 3, 3, 3)
 N_MSG = 160
 
 
@@ -233,6 +233,8 @@
 
     def comm(t):
         if t == 0:
+            crossed(0, 2)
+            crossed(1, 2)
             for m in (0, 1):
                 ring_start(m, 1, 1)
             for k in range(2):
@@ -240,6 +242,10 @@
                     second_done(m, k)
             e_ready(2)
         if t == 1:
+            crossed(0, 3)
+            crossed(1, 3)
+            ring_fwd(0, 1, 0)
+            ring_fwd(1, 1, 0)
             e_ready(3)
             for k in range(2):
                 arrived(tail_cross, k)
@@ -251,32 +257,25 @@
                         lanes = jnp.where(group == i, tb[k, half * 2 + i // 4, i % 4], lanes)
                     tv[k, :, half * 128 : half * 128 + 128] = lanes
         if t == 2:
-            ring_fwd(0, 1, 0)
-            ring_fwd(1, 1, 0)
-        if t == 3:
             ring_fwd(0, 1, 1)
             ring_fwd(1, 1, 1)
         if t == 4:
             e_ready(0)
-            crossed(0, 2)
-            crossed(1, 2)
             ring_fin(0, 1, 0)
         if t == 5:
+            ring_fwd(0, 1, 2)
+            ring_fwd(1, 1, 2)
             e_ready(1)
-            crossed(0, 3)
-            crossed(1, 3)
             ring_fin(1, 1, 0)
         if t == 6:
             ring_fin(0, 1, 1)
         if t == 7:
             ring_fin(1, 1, 1)
-            ring_fwd(0, 1, 2)
-            ring_fwd(1, 1, 2)
         if t == 8:
+            ring_fwd(0, 1, 3)
+            ring_fwd(1, 1, 3)
             crossed(2, 2)
         if t == 9:
-            ring_fwd(0, 1, 3)
-            ring_fwd(1, 1, 3)
             crossed(2, 3)
         if t == 10:
             pack(0)
@@ -287,13 +286,13 @@
         if t == 11:
             ring_fin(1, 1, 2)
         if t == 12:
+            crossed(3, 2)
+        if t == 13:
+            crossed(3, 3)
+        if t == 14:
             ring_fin(0, 1, 3)
-        if t == 13:
+        if t == 15:
             ring_fin(1, 1, 3)
-        if t == 14:
-            crossed(3, 2)
-        if t == 15:
-            crossed(3, 3)
 
     sub = lax.broadcasted_iota(jnp.int32, (8, 256), 0)
     blocks = rows // 8
@@ -421,7 +420,7 @@
 
 def build_kernel(
     head_ref, rel_ref, order_ref, tail_ref, ent_ref, table_ref, q_ref, tails_ref, wide_ref,
-    head_rows, rel_rows, qf, sem,
+    head_rows, rel_rows, relf, head_at, sem,
 ):
     rows, width = ent_ref.shape[1:]
     half_width = width // 2
@@ -442,23 +441,28 @@
         tails_ref[k] = acc
     for i in range(32):
         wide_ref[i : i + 1, :] = jnp.full((1, 128), order_ref[i], jnp.int32)
+        head_at[i : i + 1, :] = jnp.full((1, 128), lax.rem(head_ref[i], 16), jnp.int32)
     pltpu.make_async_copy(rel_rows, rel_rows, sem.at[1]).wait()
-    pltpu.make_async_copy(head_rows, head_rows, sem.at[0]).wait()
-    sub16 = lax.broadcasted_iota(jnp.int32, (16, width), 0)
-
-    def pick(i, carry):
-        hit = sub16 == lax.rem(head_ref[i], 16)
+    def spread(i, carry):
         right = rel_rows[i].astype(F32)
         for m in range(4):
-            left = jnp.sum(jnp.where(hit, head_rows[i, m].astype(F32), 0.0), axis=0, keepdims=True)
-            a, b = left[:, :half_width], left[:, half_width:]
-            c, d = right[m : m + 1, :half_width], right[m : m + 1, half_width:]
-            qf[m, pl.ds(i, 1), :half_width] = a * c - b * d
-            qf[m, pl.ds(i, 1), half_width:] = a * d + b * c
+            relf[m, pl.ds(i, 1), :] = right[m : m + 1, :]
         return carry
 
-    lax.fori_loop(0, 32, pick, 0, unroll=4)
-    q_ref[...] = qf[...].astype(BF16)
+    lax.fori_loop(0, 32, spread, 0, unroll=8)
+    pltpu.make_async_copy(head_rows, head_rows, sem.at[0]).wait()
+    lane = lax.broadcasted_iota(jnp.int32, (32, 128), 1)
+    sub = lax.broadcasted_iota(jnp.int32, (32, 128), 0)
+    inside = lax.rem(lane, 16) == head_at[...]
+    picker = jnp.concatenate(
+        [jnp.where(jnp.logical_and(inside, lane // 16 + 8 * c == sub), 1.0, 0.0) for c in range(4)], axis=1
+    ).astype(BF16)
+    for m in range(4):
+        left = jnp.dot(picker, head_rows[:, m].reshape(512, width), preferred_element_type=F32)
+        a, b = left[:, :half_width], left[:, half_width:]
+        c, d = relf[m, :, :half_width], relf[m, :, half_width:]
+        q_ref[m, :, :half_width] = (a * c - b * d).astype(BF16)
+        q_ref[m, :, half_width:] = (a * d + b * c).astype(BF16)
 
 
 def per_device(entity_table, relation_table, head_ids, relation_ids, order, tail_ids):
@@ -480,6 +484,7 @@
             pltpu.VMEM((32, members, 16, width), BF16),
             pltpu.VMEM((32, members, width), BF16),
             pltpu.VMEM((members, 32, width), F32),
+            pltpu.VMEM((32, 128), jnp.int32),
             dma((2,)),
         ],
         compiler_params=pltpu.CompilerParams(vmem_limit_bytes=58 * 1024 * 1024),

time: 73.5 us -> 70.3 us (0.956)
  Pallas kernels: 70.1 us -> 67 us
    pallas_call x1, Pallas kernels: 64.7 us -> 62.7 us  [per_device(): pl.pallas_call(score_kernel, out_shape=jax.ShapeDtypeStruct((8, 128), F32...]
    pallas_call x1, Pallas kernels: 5.41 us -> 4.22 us  [per_device(): pl.pallas_call(build_kernel, out_shape=(jax.ShapeDtypeStruct((members, 32...]
where the time goes in v5:
time: 70.3 us; the launch traced here: 70.1 us
  Pallas kernels  67 us (95%)
  local copies, waits for them, and re-layouts  2.44 us (3%)
    pallas_call x1, Pallas kernels, per_device(): pl.pallas_call(score_kernel, out_shape=jax.ShapeDtypeStruct((8, 128), F32...  62.7 us
    pallas_call x1, Pallas kernels, per_device(): pl.pallas_call(build_kernel, out_shape=(jax.ShapeDtypeStruct((members, 32...  4.22 us

profile of v5, /device:TPU:1, one launch (start us, length us, event | category | flops | bytes accessed | tf_op | source)
XLA Modules:
  0.0 70.1 jit_solution(11679612182629176905)
XLA Ops:
  0.6 4.2 %build_queries.1 = (bf16[4,32,768]{2,1,0:T(8,128)(2,1)}, s32[2,1,128]{2,1,0:T(1,128)}, s32[32,128]{1,0:T(8,128)}) custom-call(s32[32]{0:T(128)} %head_ref.1, s32[32]{0:T(128)} %rel_ref.1, s32[32]{0:T(128)} %order_ref.1, s32[32]{0:T(128)} %tail_ref.1, bf16[4,1024,768]{2,1,0:T(8,128)(2,1)} %ent_ref.3, bf16[1387,4,768]{2,1,0:T(4,128)(2,1)} %bitcast.5), custom_call_target="tpu_custom_call" | custom-call | tf_op jit(solution)/shard_map/build_queries/pallas_call | solution.py:474
  4.9 62.7 %score_exchange.1 = f32[8,128]{1,0:T(8,128)} custom-call(bf16[4,32,768]{2,1,0:T(8,128)(2,1)} %get-tuple-element.5.q_ref, s32[2,1,128]{2,1,0:T(1,128)} %get-tuple-element.6.tails_ref, s32[32,128]{1,0:T(8,128)} %get-tuple-element.7.order_ref, bf16[4,1024,768]{2,1,0:T(8,128)(2,1)} %ent_ref.3), custom_call_target="tpu_custom_call" | custom-call | flops 12884901888 | bytes 12582912 | tf_op jit(solution)/shard_map/score_exchange/pallas_call | solution.py:493
  67.6 1.2 %slice_bitcast_fusion.1 = f32[32]{0:T(128)} fusion(f32[8,128]{1,0:T(8,128)} %score_exchange.1), kind=kLoop, calls=%fused_computation.1 | loop fusion | bytes 256 | tf_op jit(solution)/shard_map/squeeze | solution.py:530
  68.8 1.3 %slice_bitcast_fusion = f32[32,4]{0,1:T(4,128)} fusion(f32[8,128]{1,0:T(8,128)} %score_exchange.1), kind=kLoop, calls=%fused_computation | loop fusion | bytes 1024 | tf_op jit(solution)/shard_map/transpose | solution.py:530

commit v6 on v5

--- a/solution.py
+++ b/solution.py
@@ -224,12 +224,16 @@
             for i in range(8):
                 rowed[half * 8 + i, k] = out[i : i + 1, :]
 
-    def send_all(n, xx, first):
+    def far_first(i):
+        order = 2 + (1 << 2) + (3 << 4)
+        return wrap(y + ((order >> (2 * (i // 4))) & 3)), wrap(z + ((order >> (2 * lax.rem(i, 4))) & 3))
+
+    def send_all(n, xx, count):
         def step(i, carry):
-            stat_copy(n, xx, wrap(y + i // 4), wrap(z + lax.rem(i, 4))).start()
+            stat_copy(n, xx, *far_first(i)).start()
             return carry
 
-        lax.fori_loop(first, 16, step, 0)
+        lax.fori_loop(0, count, step, 0)
 
     def comm(t):
         if t == 0:
@@ -263,25 +267,25 @@
             e_ready(0)
             ring_fin(0, 1, 0)
         if t == 5:
-            ring_fwd(0, 1, 2)
-            ring_fwd(1, 1, 2)
             e_ready(1)
             ring_fin(1, 1, 0)
         if t == 6:
+            ring_fwd(0, 1, 2)
+            ring_fwd(1, 1, 2)
             ring_fin(0, 1, 1)
         if t == 7:
             ring_fin(1, 1, 1)
         if t == 8:
+            crossed(2, 2)
+        if t == 9:
             ring_fwd(0, 1, 3)
             ring_fwd(1, 1, 3)
-            crossed(2, 2)
-        if t == 9:
             crossed(2, 3)
         if t == 10:
             pack(0)
             pack(1)
             pltpu.make_async_copy(rowed.at[src, pl.ds(0, 2)], r.at[src, pl.ds(0, 2)], r_recv.at[0]).start()
-            send_all(0, x, 1)
+            send_all(0, x, 15)
             ring_fin(0, 1, 2)
         if t == 11:
             ring_fin(1, 1, 2)
@@ -342,10 +346,10 @@
 
     lax.fori_loop(0, 8, batches, 0)
     pack(2)
-    send_all(1, wrap(x - 1), 0)
+    send_all(1, wrap(x - 1), 16)
     process(s1, BATCH_M[15], BATCH_K[15])
     pack(3)
-    send_all(2, wrap(x + 1), 0)
+    send_all(2, wrap(x + 1), 16)
 
     whole = (r.at[:, pl.ds(0, 2)], r.at[:, pl.ds(2, 1)], r.at[:, pl.ds(3, 1)])
     part = r.at[pl.ds(0, 15), pl.ds(0, 2)]
@@ -386,12 +390,20 @@
 
     pltpu.make_async_copy(row, g.at[idx], g_recv.at[0]).start()
 
+    mine = lax.rem(idx, 4)
+
+    def g_start(yy, zz, c):
+        to = {"ent": zz * 16 + yy * 4 + lax.rem(mine + c, 4), "rep": rep}
+        remote(row, g.at[idx], g_send.at[0], g_recv.at[0], to).start()
+
     def g_step(i, carry):
-        to = {"ent": lax.rem(idx + i, 64), "rep": rep}
-        remote(row, g.at[idx], g_send.at[0], g_recv.at[0], to).start()
+        for c in (2, 3, 1, 0):
+            g_start(*far_first(i), c)
         return carry
 
-    lax.fori_loop(1, 64, g_step, 0)
+    lax.fori_loop(0, 15, g_step, 0)
+    for c in (2, 3, 1):
+        g_start(y, z, c)
     order = order_ref[...]
     sub32 = lax.broadcasted_iota(jnp.int32, order.shape, 0)
     owner = order // 32
@@ -463,6 +475,11 @@
         c, d = relf[m, :, :half_width], relf[m, :, half_width:]
         q_ref[m, :, :half_width] = (a * c - b * d).astype(BF16)
         q_ref[m, :, half_width:] = (a * d + b * c).astype(BF16)
+
+
+def split_kernel(out_ref, ens_ref, mem_ref):
+    ens_ref[...] = out_ref[4:5, :32]
+    mem_ref[...] = out_ref[0:4, :32]
 
 
 def per_device(entity_table, relation_table, head_ids, relation_ids, order, tail_ids):
@@ -527,7 +544,14 @@
         ),
         name="score_exchange",
     )(query, tails, order_wide, entity_table)
-    return (out[4, :32], out[:4, :32].T)
+    ens, mem = pl.pallas_call(
+        split_kernel,
+        out_shape=(jax.ShapeDtypeStruct((1, 32), F32), jax.ShapeDtypeStruct((4, 32), F32)),
+        in_specs=[vmem],
+        out_specs=(vmem, vmem),
+        name="split_output",
+    )(out)
+    return (ens.reshape(32), mem.T)
 
 
 def solution(mesh):

time: 70.3 us -> 68.8 us (0.979)
  local copies, waits for them, and re-layouts: 2.44 us -> 0 us
  Pallas kernels: 67 us -> 68 us
    pallas_call x0 -> x1, Pallas kernels: none -> 1.26 us  [per_device(): pl.pallas_call(split_kernel, out_shape=(jax.ShapeDtypeStruct((1, 32), F32...]
    transpose x1 -> x0, local copies, waits for them, and re-layouts: 1.25 us -> none  [per_device(): return (out[4, :32], out[:4, :32].T)]
    squeeze x1 -> x0, local copies, waits for them, and re-layouts: 1.19 us -> none  [per_device(): return (out[4, :32], out[:4, :32].T)]
where the time goes in v6:
time: 68.8 us; the launch traced here: 68.6 us
  Pallas kernels  68 us (99%)
    pallas_call x1, Pallas kernels, per_device(): pl.pallas_call(score_kernel, out_shape=jax.ShapeDtypeStruct((8, 128), F32...  62.5 us
    pallas_call x1, Pallas kernels, per_device(): pl.pallas_call(build_kernel, out_shape=(jax.ShapeDtypeStruct((members, 32...  4.22 us

profile of v6, /device:TPU:1, one launch (start us, length us, event | category | flops | bytes accessed | tf_op | source)
XLA Modules:
  0.0 68.6 jit_solution(17862193364752083503)
XLA Ops:
  0.6 4.2 %build_queries.1 = (bf16[4,32,768]{2,1,0:T(8,128)(2,1)}, s32[2,1,128]{2,1,0:T(1,128)}, s32[32,128]{1,0:T(8,128)}) custom-call(s32[32]{0:T(128)} %head_ref.1, s32[32]{0:T(128)} %rel_ref.1, s32[32]{0:T(128)} %order_ref.1, s32[32]{0:T(128)} %tail_ref.1, bf16[4,1024,768]{2,1,0:T(8,128)(2,1)} %ent_ref.3, bf16[1387,4,768]{2,1,0:T(4,128)(2,1)} %bitcast.3), custom_call_target="tpu_custom_call" | custom-call | tf_op jit(solution)/shard_map/build_queries/pallas_call | solution.py:491
  4.9 62.5 %score_exchange.1.out_ref = f32[8,128]{1,0:T(8,128)} custom-call(bf16[4,32,768]{2,1,0:T(8,128)(2,1)} %get-tuple-element.7.q_ref, s32[2,1,128]{2,1,0:T(1,128)} %get-tuple-element.8.tails_ref, s32[32,128]{1,0:T(8,128)} %get-tuple-element.9.order_ref, bf16[4,1024,768]{2,1,0:T(8,128)(2,1)} %ent_ref.3), custom_call_target="tpu_custom_call" | custom-call | flops 12884901888 | bytes 12582912 | tf_op jit(solution)/shard_map/score_exchange/pallas_call | solution.py:510
  67.3 1.3 %split_output.1 = (f32[1,32]{1,0:T(1,128)}, f32[4,32]{1,0:T(4,128)}) custom-call(f32[8,128]{1,0:T(8,128)} %score_exchange.1.out_ref), custom_call_target="tpu_custom_call" | custom-call | tf_op jit(solution)/shard_map/split_output/pallas_call | solution.py:547

commit v7 on v6

--- a/solution.py
+++ b/solution.py
@@ -24,7 +24,7 @@
 def score_kernel(
     q_ref, tails_ref, order_ref, ent_ref, out_ref,
     u, e, s0, s1, tb, tv, stat, rowed, r, row, g,
-    send, recv, e_local, e_send, e_recv, r_send, r_recv, g_send, g_recv,
+    order_in, in_sem, send, recv, e_local, e_send, e_recv, r_send, r_recv, g_send, g_recv,
 ):
     rows, width = e.shape[2:]
     idx = lax.axis_index("ent")
@@ -58,19 +58,20 @@
     def e_copy(m):
         return remote(ent_ref.at[m], e.at[1, m], e_send.at[m], e_recv.at[m], dev(x, y, z, 1 - core))
 
-    for m in (2, 3, 0, 1):
-        e_own(m).start()
 
     barrier = pltpu.get_barrier_semaphore()
     partners = [along(axis, shift) for axis in "xyz" for shift in (1, -1)] + [dev(x, y, z, 1 - core)]
     for partner in partners:
         pl.semaphore_signal(barrier, inc=1, device_id=partner, device_id_type=MESH)
 
-    for m in range(4):
-        for k in range(2):
-            u[m, k, y, z] = q_ref[m, 16 * k : 16 * k + 16, :]
-    for k in range(2):
-        tb[k, y, z] = tails_ref[k]
+    for m in (2, 3, 0, 1):
+        for k in range(2):
+            pltpu.make_async_copy(q_ref.at[m, pl.ds(16 * k, 16)], u.at[m, k, y, z], in_sem.at[m]).start()
+    own_tails = tb.at[pl.ds(0, 2), y, z]
+    pltpu.make_async_copy(tails_ref, own_tails, in_sem.at[4]).start()
+    pltpu.make_async_copy(order_ref, order_in, in_sem.at[5]).start()
+    for m in (2, 3, 0, 1):
+        e_own(m).start()
     pl.semaphore_wait(barrier, len(partners))
 
     numbers = {}
@@ -133,7 +134,9 @@
         arrived(ring, m, ph, k, q, 2)
 
     for m in (2, 3, 0, 1):
+        pltpu.make_async_copy(q_ref.at[m], q_ref.at[m], in_sem.at[m]).wait()
         if m == 0:
+            pltpu.make_async_copy(tails_ref, own_tails, in_sem.at[4]).wait()
             for j in range(2):
                 start(tail_ring, 0, j)
         for k in range(2):
@@ -404,7 +407,8 @@
     lax.fori_loop(0, 15, g_step, 0)
     for c in (2, 3, 1):
         g_start(y, z, c)
-    order = order_ref[...]
+    pltpu.make_async_copy(order_ref, order_in, in_sem.at[5]).wait()
+    order = order_in[...]
     sub32 = lax.broadcasted_iota(jnp.int32, order.shape, 0)
     owner = order // 32
     inside = lax.rem(order // 16, 2) * 64 + lax.rem(order, 16)
@@ -510,7 +514,7 @@
     out = pl.pallas_call(
         score_kernel,
         out_shape=jax.ShapeDtypeStruct((8, 128), F32),
-        in_specs=[vmem, vmem, vmem, hbm],
+        in_specs=[hbm, hbm, hbm, hbm],
         out_specs=vmem,
         scratch_shapes=[
             pltpu.VMEM((4, 4, 4, 4, 16, width), BF16),
@@ -524,6 +528,8 @@
             pltpu.VMEM((16, 4, 1, 128), F32),
             pltpu.VMEM((1, 128), F32),
             pltpu.VMEM((64, 1, 128), F32),
+            pltpu.VMEM((32, 128), jnp.int32),
+            dma((6,)),
             dma((N_MSG,)),
             dma((N_MSG,)),
             dma((4,)),

time: 68.8 us -> 68 us (0.988)
  Pallas kernels: 68 us -> 67.2 us
    pallas_call x1, Pallas kernels: 62.5 us -> 61.7 us  [per_device(): pl.pallas_call(score_kernel, out_shape=jax.ShapeDtypeStruct((8, 128), F32...]
where the time goes in v7:
time: 68 us; the launch traced here: 67.8 us
  Pallas kernels  67.2 us (99%)
    pallas_call x1, Pallas kernels, per_device(): pl.pallas_call(score_kernel, out_shape=jax.ShapeDtypeStruct((8, 128), F32...  61.7 us
    pallas_call x1, Pallas kernels, per_device(): pl.pallas_call(build_kernel, out_shape=(jax.ShapeDtypeStruct((members, 32...  4.22 us

profile of v7, /device:TPU:1, one launch (start us, length us, event | category | flops | bytes accessed | tf_op | source)
XLA Modules:
  0.0 67.8 jit_solution(14828344473900306088)
XLA Ops:
  0.6 4.2 %build_queries.1 = (bf16[4,32,768]{2,1,0:T(8,128)(2,1)}, s32[2,1,128]{2,1,0:T(1,128)}, s32[32,128]{1,0:T(8,128)}) custom-call(s32[32]{0:T(128)} %head_ref.1, s32[32]{0:T(128)} %rel_ref.1, s32[32]{0:T(128)} %order_ref.1, s32[32]{0:T(128)} %tail_ref.1, bf16[4,1024,768]{2,1,0:T(8,128)(2,1)} %ent_ref.3, bf16[1387,4,768]{2,1,0:T(4,128)(2,1)} %bitcast.3), custom_call_target="tpu_custom_call" | custom-call | tf_op jit(solution)/shard_map/build_queries/pallas_call | solution.py:495
  4.9 61.7 %score_exchange.1.out_ref = f32[8,128]{1,0:T(8,128)} custom-call(bf16[4,32,768]{2,1,0:T(8,128)(2,1)} %get-tuple-element.7.q_ref, s32[2,1,128]{2,1,0:T(1,128)} %get-tuple-element.8.tails_ref, s32[32,128]{1,0:T(8,128)} %get-tuple-element.9.order_ref, bf16[4,1024,768]{2,1,0:T(8,128)(2,1)} %ent_ref.3), custom_call_target="tpu_custom_call" | custom-call | flops 12884901888 | bytes 12582912 | tf_op jit(solution)/shard_map/score_exchange/pallas_call | solution.py:514
  66.5 1.3 %split_output.1 = (f32[1,32]{1,0:T(1,128)}, f32[4,32]{1,0:T(4,128)}) custom-call(f32[8,128]{1,0:T(8,128)} %score_exchange.1.out_ref), custom_call_target="tpu_custom_call" | custom-call | tf_op jit(solution)/shard_map/split_output/pallas_call | solution.py:553

commit v8 on v7

--- a/solution.py
+++ b/solution.py
@@ -281,14 +281,14 @@
         if t == 8:
             crossed(2, 2)
         if t == 9:
+            pack(0)
+            pack(1)
+            pltpu.make_async_copy(rowed.at[src, pl.ds(0, 2)], r.at[src, pl.ds(0, 2)], r_recv.at[0]).start()
+            send_all(0, x, 15)
             ring_fwd(0, 1, 3)
             ring_fwd(1, 1, 3)
             crossed(2, 3)
         if t == 10:
-            pack(0)
-            pack(1)
-            pltpu.make_async_copy(rowed.at[src, pl.ds(0, 2)], r.at[src, pl.ds(0, 2)], r_recv.at[0]).start()
-            send_all(0, x, 15)
             ring_fin(0, 1, 2)
         if t == 11:
             ring_fin(1, 1, 2)
@@ -448,7 +448,7 @@
         pltpu.make_async_copy(table_ref.at[rel_ref[i]], rel_rows.at[i], sem.at[1]).start()
         return carry
 
-    lax.fori_loop(0, 32, fetch, 0, unroll=4)
+    lax.fori_loop(0, 32, fetch, 0, unroll=16)
     lane16 = lax.rem(lax.broadcasted_iota(jnp.int32, (1, 128), 1), 16)
     for k in range(2):
         acc = jnp.zeros((1, 128), jnp.int32)

time: 68 us -> 67.9 us (level)
  no operation moved by 1% of the time
where the time goes in v8:
time: 67.9 us; the launch traced here: 67.7 us
  Pallas kernels  67 us (99%)
    pallas_call x1, Pallas kernels, per_device(): pl.pallas_call(score_kernel, out_shape=jax.ShapeDtypeStruct((8, 128), F32...  61.5 us
    pallas_call x1, Pallas kernels, per_device(): pl.pallas_call(build_kernel, out_shape=(jax.ShapeDtypeStruct((members, 32...  4.21 us

profile of v8, /device:TPU:1, one launch (start us, length us, event | category | flops | bytes accessed | tf_op | source)
XLA Modules:
  0.0 67.7 jit_solution(5527121812241534847)
XLA Ops:
  0.6 4.2 %build_queries.1 = (bf16[4,32,768]{2,1,0:T(8,128)(2,1)}, s32[2,1,128]{2,1,0:T(1,128)}, s32[32,128]{1,0:T(8,128)}) custom-call(s32[32]{0:T(128)} %head_ref.1, s32[32]{0:T(128)} %rel_ref.1, s32[32]{0:T(128)} %order_ref.1, s32[32]{0:T(128)} %tail_ref.1, bf16[4,1024,768]{2,1,0:T(8,128)(2,1)} %ent_ref.3, bf16[1387,4,768]{2,1,0:T(4,128)(2,1)} %bitcast.3), custom_call_target="tpu_custom_call" | custom-call | tf_op jit(solution)/shard_map/build_queries/pallas_call | solution.py:495
  4.9 61.5 %score_exchange.1.out_ref = f32[8,128]{1,0:T(8,128)} custom-call(bf16[4,32,768]{2,1,0:T(8,128)(2,1)} %get-tuple-element.7.q_ref, s32[2,1,128]{2,1,0:T(1,128)} %get-tuple-element.8.tails_ref, s32[32,128]{1,0:T(8,128)} %get-tuple-element.9.order_ref, bf16[4,1024,768]{2,1,0:T(8,128)(2,1)} %ent_ref.3), custom_call_target="tpu_custom_call" | custom-call | flops 12884901888 | bytes 12582912 | tf_op jit(solution)/shard_map/score_exchange/pallas_call | solution.py:514
  66.4 1.3 %split_output.1 = (f32[1,32]{1,0:T(1,128)}, f32[4,32]{1,0:T(4,128)}) custom-call(f32[8,128]{1,0:T(8,128)} %score_exchange.1.out_ref), custom_call_target="tpu_custom_call" | custom-call | tf_op jit(solution)/shard_map/split_output/pallas_call | solution.py:553
